TPU v7x, 32 devices: a whole 2x2x4 slice. The times are simulated.
32 devices in a mesh: dom: 4 (over y, core), shard: 8 (over z, x).
Axes of the slice: x: 2, y: 2, z: 4, core: 2. Of those that a mesh axis runs over, the one named last changes fastest.
Arguments:
- features: bfloat16 [8192, 512], P(('dom', 'shard')), may hold values from -6 to 6
- w_self: bfloat16 [512, 512], replicated, may hold values from -0.25 to 0.25
- w_neigh: bfloat16 [512, 512], replicated, may hold values from -0.25 to 0.25
- cotangent: bfloat16 [8192, 512], P(('dom', 'shard')), may hold values from -6 to 6
- neighbours: int32 [8192, 32], P(('dom', 'shard')), may hold values from 0 to 320, as said below
- hub_slots: int32 [32], P(('dom', 'shard')), may hold values from 0 to 255, as said below
- send_rows: int32 [32, 8, 4], P(('dom', 'shard')), may hold values from 0 to 255, as said below
- send_counts: int32 [32, 8], P(('dom', 'shard')), may hold values from 1 to 4, as said below
Outputs:
- hidden: bfloat16 [8192, 512], P(('dom', 'shard'))
- grad_features: float32 [8192, 512], P(('dom', 'shard'))
- grad_self: float32 [512, 512], replicated
- grad_neigh: float32 [512, 512], replicated
Inputs may be any that keep to these rules, and one draw needn't show every extreme that they name: `neighbours`: padding slots (320) come after a vertex's live slots; each vertex has 4 to 32 live slots. A slot at or above 288 names peer p and position k with k below send_counts of that peer for this device. Hub indices are skewed: some hubs are read far more than others. `hub_slots`: the 1 entries of one device are distinct local rows. `send_rows`: rows may repeat; entries at or past a peer's count are not live. `send_counts`: in every partition group one shard index receives 4 rows from every peer.
All inputs are finite; a program needn't handle non-finite values.
Results may differ from a plain program's by a relative error of at most 0.0052.
Values may be sent and summed in bfloat16 or wider, within the bound.
A program may use at most 64 MiB of HBM per device.

v0:
```python
import jax
import jax.numpy as jnp
from jax import lax
from jax.sharding import PartitionSpec as P

row_block = 128


def contract_rows(left, right):
    return lax.dot_general(
        left, right, (((0,), (0,)), ((), ())), preferred_element_type=jnp.float32
    )


def contract_cols(left, right):
    return lax.dot_general(
        left, right, (((1,), (1,)), ((), ())), preferred_element_type=jnp.float32
    )


def body(features, w_self, w_neigh, cotangent, neighbours, hub_slots, send_rows, send_counts):
    verts, width = features.shape
    slots = neighbours.shape[1]
    peers = lax.axis_size("shard")
    routes = send_rows[0]
    counts = send_counts[0]
    cap = routes.shape[1]
    live = jnp.arange(cap)[None, :] < counts[:, None]
    hub_local = features[hub_slots]
    hubs = lax.all_gather(hub_local, ("dom", "shard"), axis=0, tiled=True)
    outgoing = jnp.where(live[:, :, None], features[routes], jnp.zeros((), jnp.bfloat16))
    incoming = lax.all_to_all(outgoing, "shard", split_axis=0, concat_axis=0, tiled=True)
    hub_count = hubs.shape[0]
    table_size = verts + hub_count + peers * cap
    table = jnp.concatenate(
        [features, hubs, incoming.reshape(peers * cap, width), jnp.zeros((1, width), jnp.bfloat16)],
        axis=0,
    )
    degree = jnp.sum(neighbours < table_size, axis=1).astype(jnp.float32)
    blocks = neighbours.reshape(verts // row_block, row_block, slots)
    sums = lax.map(lambda blk: jnp.sum(table[blk], axis=1, dtype=jnp.float32), blocks).reshape(
        verts, width
    )
    agg = (sums / degree[:, None]).astype(jnp.bfloat16)
    z = jnp.dot(features, w_self, preferred_element_type=jnp.float32) + jnp.dot(
        agg, w_neigh, preferred_element_type=jnp.float32
    )
    sig = jax.nn.sigmoid(z)
    hidden = (z * sig).astype(jnp.bfloat16)
    dz = (cotangent.astype(jnp.float32) * sig * (1.0 + z * (1.0 - sig))).astype(jnp.bfloat16)
    grad_self, grad_neigh = lax.psum(
        (contract_rows(features, dz), contract_rows(agg, dz)), ("dom", "shard")
    )
    edge_grad = contract_cols(dz, w_neigh) / degree[:, None]
    grads = edge_grad.reshape(verts // row_block, row_block, width)

    def add_block(acc, pair):
        blk, grad = pair
        spread = jnp.broadcast_to(grad[:, None, :], (row_block, slots, width)).reshape(-1, width)
        return (acc.at[blk.reshape(-1)].add(spread), None)

    start = jnp.zeros((table_size + 1, width), jnp.float32)
    accum, _ = lax.scan(add_block, start, (blocks, grads))
    hub_part = accum[verts : verts + hub_count]
    hub_back = lax.psum_scatter(hub_part, ("dom", "shard"), scatter_dimension=0, tiled=True)
    recv_part = accum[verts + hub_count : table_size].reshape(peers, cap, width)
    returned = lax.all_to_all(
        recv_part.astype(jnp.bfloat16), "shard", split_axis=0, concat_axis=0, tiled=True
    ).astype(recv_part.dtype)
    returned = jnp.where(live[:, :, None], returned, 0.0)
    grad_features = contract_cols(dz, w_self) + accum[:verts]
    grad_features = grad_features.at[hub_slots].add(hub_back)
    grad_features = grad_features.at[routes.reshape(-1)].add(returned.reshape(-1, width))
    return (hidden, grad_features, grad_self, grad_neigh)


def solution(mesh):
    return jax.shard_map(
        body,
        mesh=mesh,
        in_specs=(
            P(("dom", "shard"), None),
            P(),
            P(),
            P(("dom", "shard"), None),
            P(("dom", "shard"), None),
            P(("dom", "shard")),
            P(("dom", "shard"), None, None),
            P(("dom", "shard"), None),
        ),
        out_specs=(P(("dom", "shard"), None), P(("dom", "shard"), None), P(), P()),
        check_vma=False,
    )
```

profile of v0, /device:TPU:0, one launch (start us, length us, event | category | flops | bytes accessed | tf_op | source)
XLA Modules:
  0.0 347.5 jit_solution(12881250769295957015)
XLA Ops:
  8.1 1.6 gather_fusion.1
  11.7 7.3 %all-to-all-start = ((bf16[8,4,512]{2,1,0:T(4,128)(2,1)}), bf16[8,4,512]{2,1,0:T(4,128)(2,1)S(1)}, u32[]{:S(2)}, u32[]{:S(2)}) async-start(bf16[8,4,512]{2,1,0:T(4,128)(2,1)} %broadcast_select_fusion), calls=%async_computation | async-start | bytes 65536 | tf_op jit(solution)/shard_map/all_to_all | solution.py:32
  19.0 1.4 fusion.2
  22.7 68.1 %all-gather = bf16[32,1,512]{2,1,0:T(2,128)(2,1)S(1)} all-gather(bf16[1,1,512]{2,1,0:T(2,128)(2,1)S(1)} %dynamic-slice_bitcast_fusion.1), channel_id=1, replica_groups=mesh['dom'=4,'shard'=8] {'dom','shard'}, dimensions={0}, use_global_device_ids=true | all-gather | bytes 33792 | tf_op jit(solution)/shard_map/all_gather | solution.py:30
  91.7 1.1 maximum_maximum_fusion
  92.8 42.2 %while.22 = (s32[]{:T(128)}, f32[2,128,512]{2,1,0:T(8,128)S(1)}, s32[2,128,32]{2,1,0:T(8,128)S(1)}, bf16[321,512]{1,0:T(8,128)(2,1)S(1)}, s32[]{:T(128)}) while((s32[]{:T(128)}, f32[2,128,512]{2,1,0:T(8,128)S(1)}, s32[2,128,32]{2,1,0:T(8,128)S(1)}, bf16[321,512]{1,0:T(8,128)(2,1)S(1)}, s32[]{:T(128)}) %tuple.59), condition=%wide.region_2.3_spmd, body=%wide.region_0.0_spmd.sunk | while | flops 4145154 | bytes 13484109 | solution.py:41
  92.9 17.3 %gather_fusion = bf16[4096,512]{1,0:T(8,128)(2,1)} fusion(bf16[321,512]{1,0:T(8,128)(2,1)S(1)} %get-tuple-element.173, s32[4096]{0:T(1024)S(1)} %broadcast_clamp_fusion.2), kind=kCustom, calls=%fused_computation.clone.1 | custom fusion | bytes 8404992 | tf_op jit(solution)/shard_map/while/body/eval_jaxpr/gather | solution.py:41
  110.2 3.7 %convert_reduce_fusion.3 = f32[128,512]{1,0:T(8,128)S(1)} fusion(bf16[4096,512]{1,0:T(8,128)(2,1)} %gather_fusion), kind=kLoop, calls=%fused_computation.4.clone.1 | loop fusion | flops 4128768 | bytes 4456448 | tf_op jit(solution)/shard_map/while/body/eval_jaxpr/reduce_sum | solution.py:41
  114.1 17.3 %gather_fusion = bf16[4096,512]{1,0:T(8,128)(2,1)} fusion(bf16[321,512]{1,0:T(8,128)(2,1)S(1)} %get-tuple-element.173, s32[4096]{0:T(1024)S(1)} %broadcast_clamp_fusion.2), kind=kCustom, calls=%fused_computation.clone.1 | custom fusion | bytes 8404992 | tf_op jit(solution)/shard_map/while/body/eval_jaxpr/gather | solution.py:41
  131.3 3.7 %convert_reduce_fusion.3 = f32[128,512]{1,0:T(8,128)S(1)} fusion(bf16[4096,512]{1,0:T(8,128)(2,1)} %gather_fusion), kind=kLoop, calls=%fused_computation.4.clone.1 | loop fusion | flops 4128768 | bytes 4456448 | tf_op jit(solution)/shard_map/while/body/eval_jaxpr/reduce_sum | solution.py:41
  135.2 1.2 multiply_convert_fusion
  136.7 1.3 convolution_bitcast_fusion
  138.1 1.3 fusion.3
  139.5 61.1 %while.23 = (s32[]{:T(128)}, f32[321,512]{1,0:T(8,128)S(1)}, s32[2,128,32]{2,1,0:T(8,128)S(1)}, f32[2,128,512]{2,1,0:T(8,128)S(1)}, s32[]{:T(128)}) while((s32[]{:T(128)}, f32[321,512]{1,0:T(8,128)S(1)}, s32[2,128,32]{2,1,0:T(8,128)S(1)}, f32[2,128,512]{2,1,0:T(8,128)S(1)}, s32[]{:T(128)}) %tuple.61), condition=%wide.region_6.7_spmd, body=%wide.region_4.6_spmd.sunk | while | flops 2109442 | bytes 34455628 | solution.py:63
  139.7 4.3 %broadcast_in_dim.68 = f32[128,32,512]{2,1,0:T(8,128)} broadcast(f32[128,512]{1,0:T(8,128)S(1)} %dynamic-slice_bitcast_fusion.3), dimensions={0,2} | broadcast | bytes 8650752 | tf_op jit(solution)/shard_map/while/body/eval_jaxpr/broadcast_in_dim | solution.py:59
  144.0 26.0 %scatter_fusion = f32[321,512]{1,0:T(8,128)S(1)} fusion(f32[321,512]{1,0:T(8,128)S(1)} %get-tuple-element.181, s32[4096]{0:T(1024)S(1)} %bitcast.62, f32[4096,512]{1,0:T(8,128)} %bitcast.59), kind=kCustom, calls=%fused_computation.2.clone.1 | custom fusion | flops 2097152 | bytes 25182208 | tf_op jit(solution)/shard_map/while/body/eval_jaxpr/scatter-add | solution.py:60
  170.2 4.3 %broadcast_in_dim.68 = f32[128,32,512]{2,1,0:T(8,128)} broadcast(f32[128,512]{1,0:T(8,128)S(1)} %dynamic-slice_bitcast_fusion.3), dimensions={0,2} | broadcast | bytes 8650752 | tf_op jit(solution)/shard_map/while/body/eval_jaxpr/broadcast_in_dim | solution.py:59
  174.5 26.1 %scatter_fusion = f32[321,512]{1,0:T(8,128)S(1)} fusion(f32[321,512]{1,0:T(8,128)S(1)} %get-tuple-element.181, s32[4096]{0:T(1024)S(1)} %bitcast.62, f32[4096,512]{1,0:T(8,128)} %bitcast.59), kind=kCustom, calls=%fused_computation.2.clone.1 | custom fusion | flops 2097152 | bytes 25182208 | tf_op jit(solution)/shard_map/while/body/eval_jaxpr/scatter-add | solution.py:60
  202.8 3.3 all-to-all-start.1
  206.5 6.5 %all-to-all-done.1 = bf16[8,4,512]{2,1,0:T(4,128)(2,1)S(1)} async-done(((bf16[8,4,512]{2,1,0:T(4,128)(2,1)}), bf16[8,4,512]{2,1,0:T(4,128)(2,1)S(1)}, u32[]{:S(2)}, u32[]{:S(2)}) %all-to-all-start.1) | async-done | bytes 32800 | tf_op jit(solution)/shard_map/all_to_all | solution.py:67
  213.2 120.1 %all-reduce.4.cloned.1.call-done = (f32[32,512]{1,0:T(8,128)}, f32[512,512]{0,1:T(8,128)}, f32[512,512]{1,0:T(8,128)}) async-done(((f32[32,512]{1,0:T(8,128)}, f32[512,512]{0,1:T(8,128)}, f32[512,512]{1,0:T(8,128)}), (f32[32,512]{1,0:T(8,128)}, f32[512,512]{0,1:T(8,128)}, f32[512,512]{1,0:T(8,128)})) %all-reduce.4.cloned.1.call-update) | async-done | bytes 2162704
  333.3 1.3 broadcast_select_fusion.1
  334.7 2.5 copy.27
  338.2 2.5 copy.51
  (71 shorter events, 10.1 us)
Async XLA Ops:
  7.2 128.0 %copy-start = (bf16[512,512]{1,0:T(8,128)(2,1)S(1)}, bf16[512,512]{1,0:T(8,128)(2,1)}, u32[]{:S(2)}) copy-start(bf16[512,512]{1,0:T(8,128)(2,1)} %param.16) | copy-start | bytes 1572868
  10.5 0.6 copy-start.7
  11.7 79.9 %all-to-all-start = ((bf16[8,4,512]{2,1,0:T(4,128)(2,1)}), bf16[8,4,512]{2,1,0:T(4,128)(2,1)S(1)}, u32[]{:S(2)}, u32[]{:S(2)}) async-start(bf16[8,4,512]{2,1,0:T(4,128)(2,1)} %broadcast_select_fusion), calls=%async_computation | async-start | bytes 65536 | tf_op jit(solution)/shard_map/all_to_all | solution.py:32
  19.0 314.3 %all-reduce.4.cloned.1.call-start = ((), (), s32[]{:S(2)}) async-start(), calls=%async_computation.2 | async-start | bytes 4325376
  92.8 42.4 %copy-start.10 = (bf16[256,512]{1,0:T(8,128)(2,1)S(1)}, bf16[256,512]{1,0:T(8,128)(2,1)}, u32[]{:S(2)}) copy-start(bf16[256,512]{1,0:T(8,128)(2,1)} %param.17) | copy-start | bytes 786436
  92.8 43.9 %copy-start.1 = (bf16[256,512]{1,0:T(8,128)(2,1)S(1)}, bf16[256,512]{1,0:T(8,128)(2,1)}, u32[]{:S(2)}) copy-start(bf16[256,512]{1,0:T(8,128)(2,1)} %param.14) | copy-start | bytes 786436
  136.4 2.9 copy-start.2
  139.4 61.9 %copy-start.6 = (s32[1,8,4]{1,2,0:T(4,128)S(1)}, s32[1,8,4]{1,2,0:T(4,128)}, u32[]{:S(2)}) copy-start(s32[1,8,4]{1,2,0:T(4,128)} %param.20) | copy-start | bytes 388
  139.4 62.0 %copy-start.9 = (s32[2]{0:T(128)S(1)}, s32[2]{0:T(128)}, u32[]{:S(2)}) copy-start(s32[2]{0:T(128)} %constant.67.clone.1) | copy-start | bytes 28
  139.4 66.7 %copy-start.3 = (bf16[256,512]{1,0:T(8,128)(2,1)S(1)}, bf16[256,512]{1,0:T(8,128)(2,1)}, u32[]{:S(2)}) copy-start(bf16[256,512]{1,0:T(8,128)(2,1)} %copy-done.2) | copy-start | bytes 786436
  139.5 66.7 %copy-start.5 = (bf16[512,512]{1,0:T(8,128)(2,1)S(1)}, bf16[512,512]{1,0:T(8,128)(2,1)}, u32[]{:S(2)}) copy-start(bf16[512,512]{1,0:T(8,128)(2,1)} %param.15) | copy-start | bytes 1572868
  139.5 73.6 %copy-start.8 = (pred[8,4]{1,0:T(8,128)(4,1)S(1)}, pred[8,4]{1,0:T(8,128)(4,1)}, u32[]{:S(2)}) copy-start(pred[8,4]{1,0:T(8,128)(4,1)} %copy-done.7) | copy-start | bytes 100
  202.8 10.2 %all-to-all-start.1 = ((bf16[8,4,512]{2,1,0:T(4,128)(2,1)}), bf16[8,4,512]{2,1,0:T(4,128)(2,1)S(1)}, u32[]{:S(2)}, u32[]{:S(2)}) async-start(bf16[8,4,512]{2,1,0:T(4,128)(2,1)} %convert_element_type.38), calls=%async_computation.1 | async-start | bytes 65536 | tf_op jit(solution)/shard_map/all_to_all | solution.py:67
  338.2 2.5 copy-start.4
Sparse Core Ops, SparseCore 0:
  201.4 131.8 all-reduce.3
where the time goes:
time: 348 us
  waiting for transfers between devices  127 us (36%)
  blocking collectives  68.1 us (20%)
  other arithmetic  66.8 us (19%)
  local copies, waits for them, and re-layouts  54.2 us (16%)
  between operations  15 us (4%)
  starting transfers between devices  10.6 us (3%)
  matrix products  5.88 us (2%)
    unnamed x2, waiting for transfers between devices  120 us
    all_gather x1, blocking collectives, body(): hubs = lax.all_gather(hub_local, ('dom', 'shard'), axis=0, tiled=True)  68.1 us
    scatter-add x2, other arithmetic, add_block(): return (acc.at[blk.reshape(-1)].add(spread), None)  52.1 us
    gather x2, local copies, waits for them, and re-layouts, body(): table[blk]  34.5 us
    broadcast_in_dim x4, local copies, waits for them, and re-layouts, add_block(): jnp.broadcast_to(grad[:, None, :], (row_block, slots, width))  8.67 us
    reduce_sum x2, other arithmetic, body(): jnp.sum(table[blk], axis=1, dtype=jnp.float32)  7.37 us
    unnamed x28, local copies, waits for them, and re-layouts  7.26 us
    all_to_all x1, starting transfers between devices, body(): lax.all_to_all(outgoing, 'shard', split_axis=0, concat_axis=0, tiled=True)  7.25 us
  transfers between devices with their start and end apart: 3, of which 2 were waited for; matrix products, arithmetic and copies ran while one was open for 2% of the time, Pallas kernels for 0%

commit v1 on v0

v1 whole, which is shorter than its diff:
```python
import jax
import jax.numpy as jnp
from jax import lax
from jax.sharding import PartitionSpec as P

BF = jnp.bfloat16


def contract_rows(left, right):
    return lax.dot_general(
        left, right, (((0,), (0,)), ((), ())), preferred_element_type=jnp.float32
    )


def contract_cols(left, right):
    return lax.dot_general(
        left, right, (((1,), (1,)), ((), ())), preferred_element_type=jnp.float32
    )


def body(features, w_self, w_neigh, cotangent, neighbours, hub_slots, send_rows, send_counts):
    verts, width = features.shape
    slots = neighbours.shape[1]
    peers = lax.axis_size("shard")
    devices = peers * lax.axis_size("dom")
    routes = send_rows[0]
    counts = send_counts[0]
    cap = routes.shape[1]
    live = jnp.arange(cap)[None, :] < counts[:, None]
    hubs_own = hub_slots.shape[0]
    hub_count = hubs_own * devices
    picks = jnp.concatenate([hub_slots, jnp.where(live, routes, verts).reshape(-1)])
    pick = (picks[:, None] == jnp.arange(verts)[None, :]).astype(BF)
    picked = jnp.dot(pick, features, preferred_element_type=jnp.float32).astype(BF)
    hubs = lax.all_gather(picked[:hubs_own], ("dom", "shard"), axis=0, tiled=True)
    outgoing = picked[hubs_own:].reshape(peers, cap, width)
    incoming = lax.all_to_all(outgoing, "shard", split_axis=0, concat_axis=0, tiled=True)
    table_size = verts + hub_count + peers * cap
    table = jnp.concatenate([features, hubs, incoming.reshape(peers * cap, width)], axis=0)
    degree = jnp.sum(neighbours < table_size, axis=1).astype(jnp.float32)
    names = jnp.arange(table_size)[None, :]
    count = jnp.zeros((verts, table_size), jnp.float32)
    for j in range(slots):
        count = count + (neighbours[:, j : j + 1] == names)
    count = count.astype(BF)
    sums = jnp.dot(count, table, preferred_element_type=jnp.float32)
    agg = (sums / degree[:, None]).astype(BF)
    z = jnp.dot(features, w_self, preferred_element_type=jnp.float32) + jnp.dot(
        agg, w_neigh, preferred_element_type=jnp.float32
    )
    sig = jax.nn.sigmoid(z)
    hidden = (z * sig).astype(BF)
    dz = (cotangent.astype(jnp.float32) * sig * (1.0 + z * (1.0 - sig))).astype(BF)
    both = jnp.concatenate([contract_rows(features, dz), contract_rows(agg, dz)], axis=0).astype(BF)
    parts = lax.all_to_all(
        both.reshape(devices, -1, width), ("dom", "shard"), split_axis=0, concat_axis=0, tiled=True
    )
    mine = jnp.sum(parts.astype(jnp.float32), axis=0).astype(BF)
    edge_grad = (contract_cols(dz, w_neigh) / degree[:, None]).astype(BF)
    accum = contract_rows(count, edge_grad)
    hub_part = accum[verts : verts + hub_count]
    hub_back = lax.psum_scatter(hub_part, ("dom", "shard"), scatter_dimension=0, tiled=True)
    recv_part = accum[verts + hub_count :].reshape(peers, cap, width)
    returned = lax.all_to_all(recv_part.astype(BF), "shard", split_axis=0, concat_axis=0, tiled=True)
    back = jnp.concatenate([hub_back.astype(BF), returned.reshape(-1, width)], axis=0)
    grad_features = contract_cols(dz, w_self) + accum[:verts] + contract_rows(pick, back)
    total = lax.all_gather(mine, ("dom", "shard"), axis=0, tiled=True).astype(jnp.float32)
    return (hidden, grad_features, total[:width], total[width:])


def solution(mesh):
    return jax.shard_map(
        body,
        mesh=mesh,
        in_specs=(
            P(("dom", "shard"), None),
            P(),
            P(),
            P(("dom", "shard"), None),
            P(("dom", "shard"), None),
            P(("dom", "shard")),
            P(("dom", "shard"), None, None),
            P(("dom", "shard"), None),
        ),
        out_specs=(P(("dom", "shard"), None), P(("dom", "shard"), None), P(), P()),
        check_vma=False,
    )
```

time: 348 us -> 186 us (0.53)
  waiting for transfers between devices: 127 us -> 3.83 us
  blocking collectives: 68.1 us -> 138 us
  other arithmetic: 66.8 us -> 1.68 us
  local copies, waits for them, and re-layouts: 54.2 us -> 7.19 us
    unnamed x2 -> x1, waiting for transfers between devices: 120 us -> 0.02 us
    scatter-add x3 -> x0, other arithmetic: 53.1 us -> none  [the longest x2 52.1 us: add_block(): return (acc.at[blk.reshape(-1)].add(spread), None)]
    unnamed x0 -> x1, blocking collectives: none -> 40.3 us
    gather x4 -> x0, local copies, waits for them, and re-layouts: 36.2 us -> none  [the longest x2 34.5 us: body(): table[blk]]
    all_to_all x0 -> x1, blocking collectives: none -> 29.3 us  [body(): lax.all_to_all(both.reshape(devices, -1, width), ('dom', 'shard'), split_...]
    broadcast_in_dim x5 -> x0, local copies, waits for them, and re-layouts: 8.73 us -> none  [the longest x4 8.67 us: add_block(): jnp.broadcast_to(grad[:, None, :], (row_block, slots, width))]
    reduce_sum x2 -> x1, other arithmetic: 7.37 us -> 0.77 us  [body(): mine = jnp.sum(parts.astype(jnp.float32), axis=0).astype(BF)]
    all_to_all x1, waiting for transfers between devices: 6.55 us -> 0.01 us  [body(): lax.all_to_all(recv_part.astype(BF), 'shard', split_axis=0, concat_axis=0...]
  transfers between devices with their start and end apart: 3 -> 3, of which waited for: 2 -> 1; matrix products, arithmetic and copies ran while one was open for 2% -> 4% of each run, Pallas kernels for 0% -> 0%
where the time goes in v1:
time: 186 us; the launch traced here: 185 us
  blocking collectives  138 us (74%)
  between operations  14.9 us (8%)
  starting transfers between devices  10.6 us (6%)
  matrix products  9.33 us (5%)
  local copies, waits for them, and re-layouts  7.19 us (4%)
  waiting for transfers between devices  3.83 us (2%)
    all_gather x1, blocking collectives, body(): lax.all_gather(picked[:hubs_own], ('dom', 'shard'), axis=0, tiled=True)  68.1 us
    unnamed x1, blocking collectives  40.3 us
    all_to_all x1, blocking collectives, body(): lax.all_to_all(both.reshape(devices, -1, width), ('dom', 'shard'), split_...  29.3 us
    all_to_all x1, starting transfers between devices, body(): lax.all_to_all(outgoing, 'shard', split_axis=0, concat_axis=0, tiled=True)  7.25 us
    all_gather x1, waiting for transfers between devices, body(): lax.all_gather(mine, ('dom', 'shard'), axis=0, tiled=True)  3.81 us
  transfers between devices with their start and end apart: 3, of which 1 were waited for; matrix products, arithmetic and copies ran while one was open for 4% of the time, Pallas kernels for 0%

profile of v1, /device:TPU:0, one launch (start us, length us, event | category | flops | bytes accessed | tf_op | source)
XLA Modules:
  0.0 185.4 jit_solution(4578518434027105139)
XLA Ops:
  7.2 0.8 copy.15
  8.1 0.7 iota_compare_fusion.35
  8.9 0.1 lt.29
  9.7 1.1 convolution_convert_fusion.2
  10.9 0.6 reshape.32
  11.5 7.3 %all-to-all-start = ((bf16[8,4,512]{2,1,0:T(4,128)(2,1)}), bf16[8,4,512]{2,1,0:T(4,128)(2,1)S(1)}, u32[]{:S(2)}, u32[]{:S(2)}) async-start(bf16[8,4,512]{2,1,0:T(4,128)(2,1)} %reshape.32), calls=%async_computation | async-start | bytes 65536 | tf_op jit(solution)/shard_map/all_to_all | solution.py:37
  18.8 1.0 fusion.18
  19.8 1.0 fusion.19
  20.8 68.1 %all-gather = bf16[32,1,512]{2,1,0:T(2,128)(2,1)S(1)} all-gather(bf16[1,1,512]{2,1,0:T(2,128)(2,1)S(1)} %slice_bitcast_fusion), channel_id=1, replica_groups=mesh['dom'=4,'shard'=8] {'dom','shard'}, dimensions={0}, use_global_device_ids=true | all-gather | bytes 33792 | tf_op jit(solution)/shard_map/all_gather | solution.py:35
  88.9 1.2 fusion.20
  90.3 1.7 fusion.2
  92.1 1.2 multiply_convert_fusion
  93.3 0.3 convolution_convert_fusion
  93.6 0.3 fusion
  94.0 29.3 %all_to_all.15 = bf16[32,32,512]{2,1,0:T(8,128)(2,1)S(1)} all-to-all(bf16[32,32,512]{2,1,0:T(8,128)(2,1)S(1)} %bitcast.54), channel_id=1, replica_groups=mesh['dom'=4,'shard'=8] {'dom','shard'}, dimensions={0} | all-to-all | bytes 2097152 | tf_op jit(solution)/shard_map/all_to_all | solution.py:55
  123.3 0.8 reduce_sum.22
  124.1 1.9 %fusion.3 = f32[320,512]{1,0:T(8,128)S(1)} fusion(bf16[256,512]{1,0:T(8,128)(2,1)S(1)} %get-tuple-element.6, bf16[512,512]{1,0:T(8,128)(2,1)S(1)} %copy-done, f32[256]{0:T(256)S(1)} %convert_element_type.180, s32[256]{0:T(256)S(1)} %bitcast.119, s32[256]{0:T(256)S(1)} %bitcast.59, s32[256]{0:T(256)S(1)} %bitcast.61, s32[256]{0:T(256)S(1)} %bitcast.63, ...), kind=kOutput, calls=%fused_computation.10 | convolution fusion | flops 226230272 | bytes 1475584 | tf_op jit(solution)/shard_map/dot_general | solution.py:10
  126.1 0.6 convert_element_type.187
  126.7 3.3 %all-to-all-start.1 = ((bf16[8,4,512]{2,1,0:T(4,128)(2,1)}), bf16[8,4,512]{2,1,0:T(4,128)(2,1)S(1)}, u32[]{:S(2)}, u32[]{:S(2)}) async-start(bf16[8,4,512]{2,1,0:T(4,128)(2,1)} %convert_element_type.187), calls=%async_computation.1 | async-start | bytes 65536 | tf_op jit(solution)/shard_map/all_to_all | solution.py:64
  130.0 40.3 %all-reduce = bf16[32,512]{1,0:T(8,128)(2,1)S(1)} all-reduce(f32[32,512]{1,0:T(8,128)S(1)} %slice.160), channel_id=2, replica_groups=mesh['dom'=4,'shard'=8] {'dom','shard'}, use_global_device_ids=true, to_apply=%region_1.2.clone | all-reduce | flops 16384 | bytes 98304
  170.4 0.3 convolution_add_fusion.1
  170.8 1.1 convolution_add_fusion
  171.9 3.8 %all-gather.3.cloned.1.call-done = bf16[1024,512]{1,0:T(8,128)(2,1)} async-done(((bf16[32,512]{1,0:T(8,128)(2,1)}), bf16[1024,512]{1,0:T(8,128)(2,1)}) %all-gather.3.cloned.1.call-update) | async-done | bytes 1048592 | tf_op jit(solution)/shard_map/all_gather | solution.py:67
  175.7 2.8 %fusion.17 = (f32[512,512]{1,0:T(8,128)}, f32[512,512]{1,0:T(8,128)}) fusion(bf16[1024,512]{1,0:T(8,128)(2,1)} %all-gather.3.cloned.1.call-done), kind=kLoop, calls=%fused_computation.71 | loop fusion | bytes 4194304 | tf_op jit(solution)/shard_map/slice | solution.py:68
  (28 shorter events, 0.4 us)
Async XLA Ops:
  7.2 84.9 %copy-start = (bf16[512,512]{1,0:T(8,128)(2,1)S(1)}, bf16[512,512]{1,0:T(8,128)(2,1)}, u32[]{:S(2)}) copy-start(bf16[512,512]{1,0:T(8,128)(2,1)} %param.10) | copy-start | bytes 1572868
  7.2 83.0 %copy-start.3 = (s32[256,32]{0,1:T(8,128)S(1)}, s32[256,32]{0,1:T(8,128)}, u32[]{:S(2)}) copy-start(s32[256,32]{0,1:T(8,128)} %param.12) | copy-start | bytes 98308
  7.2 81.7 %copy-start.2 = (bf16[512,512]{1,0:T(8,128)(2,1)S(1)}, bf16[512,512]{1,0:T(8,128)(2,1)}, u32[]{:S(2)}) copy-start(bf16[512,512]{1,0:T(8,128)(2,1)} %param.9) | copy-start | bytes 1572868
  10.8 79.4 %copy-start.1 = (bf16[256,512]{1,0:T(8,128)(2,1)S(1)}, bf16[256,512]{1,0:T(8,128)(2,1)}, u32[]{:S(2)}) copy-start(bf16[256,512]{1,0:T(8,128)(2,1)} %param.8) | copy-start | bytes 786436
  11.5 78.8 %all-to-all-start = ((bf16[8,4,512]{2,1,0:T(4,128)(2,1)}), bf16[8,4,512]{2,1,0:T(4,128)(2,1)S(1)}, u32[]{:S(2)}, u32[]{:S(2)}) async-start(bf16[8,4,512]{2,1,0:T(4,128)(2,1)} %reshape.32), calls=%async_computation | async-start | bytes 65536 | tf_op jit(solution)/shard_map/all_to_all | solution.py:37
  18.7 157.0 %all-gather.3.cloned.1.call-start = ((), (), s32[]{:S(2)}) async-start(), calls=%async_computation.3 | async-start | bytes 1081344 | tf_op jit(solution)/shard_map/all_gather | solution.py:67
  90.3 1.8 copy-start.4
  126.7 44.1 %all-to-all-start.1 = ((bf16[8,4,512]{2,1,0:T(4,128)(2,1)}), bf16[8,4,512]{2,1,0:T(4,128)(2,1)S(1)}, u32[]{:S(2)}, u32[]{:S(2)}) async-start(bf16[8,4,512]{2,1,0:T(4,128)(2,1)} %convert_element_type.187), calls=%async_computation.1 | async-start | bytes 65536 | tf_op jit(solution)/shard_map/all_to_all | solution.py:64
Sparse Core Ops, SparseCore 0:
  124.3 51.4 all-gather.2

commit v2 on v1

v2 whole, which is shorter than its diff:
```python
import functools

import jax
import jax.numpy as jnp
from jax import lax
from jax.experimental import pallas as pl
from jax.experimental.pallas import tpu as pltpu
from jax.sharding import PartitionSpec as P

BF = jnp.bfloat16
F32 = jnp.float32
MESH = pl.DeviceIdType.MESH
COLUMN_PARTS = 1
ROW_TILE = 16


def contract_rows(left, right):
    return lax.dot_general(left, right, (((0,), (0,)), ((), ())), preferred_element_type=F32)


def contract_cols(left, right):
    return lax.dot_general(left, right, (((1,), (1,)), ((), ())), preferred_element_type=F32)


def dot(left, right):
    return jnp.dot(left, right, preferred_element_type=F32)


def round_up(value, step):
    return -(-value // step) * step


def kernel(
    nd, ns,
    features, w_self, w_neigh, cotangent, neighbours, hub_slots, send_rows, send_counts,
    hidden, grad_features, grad_self, grad_neigh,
    pick, picked, hub_out, hub_in, bound_out, bound_in, table, count, agg, zs, dz, eg, accum,
    hub_send, hub_back, bound_send, bound_back, back,
    s1, r1, acc1, s2, r2, acc2, s3, r3, gathered,
    small_send, small_recv, send_sems, recv_sems,
):
    verts, width = features.shape
    slots = neighbours.shape[1]
    devices = nd * ns
    cap = send_rows.shape[2]
    hubs_own = hub_slots.shape[0]
    hub_count = hubs_own * devices
    live_rows = hub_count + ns * cap
    table_size = verts + live_rows
    dom = lax.axis_index("dom")
    shard = lax.axis_index("shard")
    me = dom * ns + shard
    core = lax.rem(dom, 2)
    y = lax.div(dom, 2)
    low = lax.rem(shard, 2)
    high = lax.div(shard, 2)

    def device_of(index):
        return (lax.div(index, ns), lax.rem(index, ns))

    barrier = pltpu.get_barrier_semaphore()

    def greet(k, carry):
        pl.semaphore_signal(
            barrier, inc=1, device_id=device_of(lax.rem(me + k, devices)), device_id_type=MESH
        )
        return carry

    lax.fori_loop(1, devices, greet, 0)

    lane = lax.broadcasted_iota(jnp.int32, (1, verts), 1)
    pick[...] = jnp.zeros_like(pick)
    for p in range(ns):
        for k in range(cap):
            row = jnp.where(k < send_counts[0, p], send_rows[0, p, k], -1)
            pick[pl.ds(p * cap + k, 1), :] = (lane == row).astype(F32)
    for h in range(hubs_own):
        pick[pl.ds(ns * cap + h, 1), :] = (lane == hub_slots[h]).astype(F32)
    picked[...] = dot(pick[...].astype(BF), features[...])
    for p in range(ns):
        bound_out[p] = picked[pl.ds(p * cap, cap), :]
    hub_out[...] = picked[pl.ds(ns * cap, hubs_own), :]

    pl.semaphore_wait(barrier, devices - 1)

    def hub_copy(k):
        return pltpu.make_async_remote_copy(
            src_ref=hub_out,
            dst_ref=hub_in.at[k - 1],
            send_sem=small_send.at[0],
            recv_sem=small_recv.at[0],
            device_id=device_of(lax.rem(me + k, devices)),
            device_id_type=MESH,
        )

    def hub_return(k):
        target = lax.rem(me + k, devices)
        return pltpu.make_async_remote_copy(
            src_ref=hub_send.at[target],
            dst_ref=hub_back.at[k - 1],
            send_sem=small_send.at[1],
            recv_sem=small_recv.at[1],
            device_id=device_of(target),
            device_id_type=MESH,
        )

    def bound_copy(source, landing, number):
        def make(k):
            target = lax.rem(shard + k, ns)
            return pltpu.make_async_remote_copy(
                src_ref=source.at[target],
                dst_ref=landing.at[k - 1],
                send_sem=small_send.at[number],
                recv_sem=small_recv.at[number],
                device_id=(dom, target),
                device_id_type=MESH,
            )

        return make

    def start_all(make, total):
        def one(k, carry):
            make(k).start()
            return carry

        lax.fori_loop(1, total, one, 0)

    def wait_all(landing, number):
        pltpu.make_async_copy(landing, landing, small_recv.at[number]).wait()
        pltpu.make_async_copy(landing, landing, small_send.at[number]).wait()

    start_all(bound_copy(bound_out, bound_in, 2), ns)
    start_all(hub_copy, devices)

    block = 32
    columns = count.shape[1]
    names = lax.broadcasted_iota(jnp.int32, (block, columns), 1)

    def count_block(i, carry):
        rows = pl.ds(pl.multiple_of(i * block, block), block)
        slot = neighbours[rows, :]
        total = jnp.zeros((block, columns), F32)
        for j in range(slots):
            total = total + (slot[:, j : j + 1] == names).astype(F32)
        count[rows, :] = total.astype(BF)
        return carry

    lax.fori_loop(0, verts // block, count_block, 0)
    degree = jnp.sum((neighbours[...] < table_size).astype(F32), axis=1, keepdims=True)
    zs[...] = dot(features[...], w_self[...])
    local_sums = dot(count[:, :verts], features[...])

    table[...] = jnp.zeros_like(table)
    for h in range(hubs_own):
        table[pl.ds(me * hubs_own + h, 1), :] = hub_out[pl.ds(h, 1), :]
    for k in range(cap):
        table[pl.ds(hub_count + shard * cap + k, 1), :] = bound_out[shard, pl.ds(k, 1), :]
    wait_all(bound_in, 2)
    for k in range(1, ns):
        source = lax.rem(shard - k + ns, ns)
        for i in range(cap):
            table[pl.ds(hub_count + source * cap + i, 1), :] = bound_in[k - 1, pl.ds(i, 1), :]
    wait_all(hub_in, 0)

    def place_hub(k, carry):
        source = lax.rem(me - k + devices, devices)
        for h in range(hubs_own):
            table[pl.ds(source * hubs_own + h, 1), :] = hub_in[k - 1, pl.ds(h, 1), :]
        return carry

    lax.fori_loop(1, devices, place_hub, 0)

    sums = local_sums + dot(count[:, verts:], table[...].astype(BF))
    agg[...] = (sums / degree).astype(BF)
    z = zs[...] + dot(agg[...], w_neigh[...])
    sig = jax.nn.sigmoid(z)
    hidden[...] = (z * sig).astype(BF)
    dz[...] = (cotangent[...].astype(F32) * sig * (1.0 + z * (1.0 - sig))).astype(BF)

    part = width // COLUMN_PARTS
    pieces = 2 * COLUMN_PARTS
    plane = (nd // 2) * 2
    tall = ns // 2
    half = width // 2
    rows2 = half // plane
    scatter = rows2 % (tall * ROW_TILE) == 0
    rows3 = rows2 // tall if scatter else rows2
    my_plane = y * 2 + low
    base1 = core * half
    base2 = base1 + my_plane * rows2
    base3 = base2 + high * rows3 if scatter else base2

    def at_core(j):
        return (y * 2 + j, shard)

    def at_plane(j):
        return (lax.div(j, 2) * 2 + core, high * 2 + lax.rem(j, 2))

    def at_tall(j):
        return (dom, j * 2 + low)

    def copy(q, stage, k, source, landing, target):
        return pltpu.make_async_remote_copy(
            src_ref=source,
            dst_ref=landing,
            send_sem=send_sems.at[q, stage, k - 1],
            recv_sem=recv_sems.at[q, stage, k - 1],
            device_id=target,
            device_id_type=MESH,
        )

    def rows_at(start, size):
        return pl.ds(pl.multiple_of(start, ROW_TILE), size)

    def left_of(q):
        return features if q // COLUMN_PARTS == 0 else agg

    def right_of(q):
        return dz[:, pl.ds((q % COLUMN_PARTS) * part, part)]

    def stage0(q):
        other = pl.ds(pl.multiple_of((1 - core) * half, half), half)
        own = pl.ds(pl.multiple_of(core * half, half), half)
        s1[q] = contract_rows(left_of(q)[:, other], right_of(q)).astype(BF)
        c = copy(q, 0, 1, s1.at[q], r1.at[q], at_core(1 - core))
        c.start()
        acc1[q] = contract_rows(left_of(q)[:, own], right_of(q))
        return [c]

    def stage1(q):
        acc1[q] = acc1[q] + r1[q].astype(F32)
        copies = []
        for k in range(1, plane):
            j = lax.rem(my_plane + k, plane)
            s2[q, k - 1] = acc1[q, rows_at(j * rows2, rows2), :].astype(BF)
            c = copy(q, 1, k, s2.at[q, k - 1], r2.at[q, k - 1], at_plane(j))
            c.start()
            copies.append(c)
        return copies

    def stage2(q):
        total = acc1[q, rows_at(my_plane * rows2, rows2), :]
        for k in range(1, plane):
            total = total + r2[q, k - 1].astype(F32)
        acc2[q] = total
        copies = []
        if not scatter:
            r3[q, high] = total.astype(BF)
        for k in range(1, tall):
            j = lax.rem(high + k, tall)
            if scatter:
                s3[q, k - 1] = acc2[q, rows_at(j * rows3, rows3), :].astype(BF)
                c = copy(q, 2, k, s3.at[q, k - 1], r3.at[q, k - 1], at_tall(j))
            else:
                c = copy(q, 2, k, r3.at[q, high], r3.at[q, high], at_tall(j))
            c.start()
            copies.append(c)
        return copies

    def stage3(q):
        if scatter:
            total = acc2[q, rows_at(high * rows3, rows3), :]
            for k in range(1, tall):
                total = total + r3[q, k - 1].astype(F32)
        else:
            total = r3[q, 0].astype(F32)
            for j in range(1, tall):
                total = total + r3[q, j].astype(F32)
        gathered[q, rows_at(base3, rows3), :] = total.astype(BF)
        copies = []
        if scatter:
            chunk = gathered.at[q, rows_at(base3, rows3), :]
            for k in range(1, tall):
                c = copy(q, 3, k, chunk, chunk, at_tall(lax.rem(high + k, tall)))
                c.start()
                copies.append(c)
        return copies

    def stage4(q):
        chunk = gathered.at[q, rows_at(base2, rows2), :]
        copies = []
        for k in range(1, plane):
            c = copy(q, 4, k, chunk, chunk, at_plane(lax.rem(my_plane + k, plane)))
            c.start()
            copies.append(c)
        return copies

    def stage5(q):
        chunk = gathered.at[q, rows_at(base1, half), :]
        c = copy(q, 5, 1, chunk, chunk, at_core(1 - core))
        c.start()
        return [c]

    def finish(copies):
        for c in copies:
            c.wait()

    stages = [stage0, stage1, stage2, stage3, stage4, stage5]
    flying = [stage0(q) for q in range(pieces)]
    for number in range(1, len(stages)):
        for q in range(pieces):
            finish(flying[q])
            flying[q] = stages[number](q)
            if number == 1 and q == 0:
                eg[...] = (contract_cols(dz[...], w_neigh[...]) / degree).astype(BF)
                accum[...] = contract_rows(count[:, verts:], eg[...])

                def fill(d, carry):
                    for h in range(hubs_own):
                        hub_send[d, pl.ds(h, 1), :] = accum[pl.ds(d * hubs_own + h, 1), :]
                    return carry

                lax.fori_loop(0, devices, fill, 0)
                for p in range(ns):
                    bound_send[p] = accum[pl.ds(hub_count + p * cap, cap), :]
                start_all(bound_copy(bound_send, bound_back, 3), ns)
                start_all(hub_return, devices)
            if number == 2 and q == 0:
                grad_features[...] = contract_cols(dz[...], w_self[...]) + contract_rows(
                    count[:, :verts], eg[...]
                )
            if number == 4 and q == pieces - 1:
                back[...] = jnp.zeros_like(back)
                for i in range(cap):
                    back[pl.ds(shard * cap + i, 1), :] = bound_send[shard, pl.ds(i, 1), :]
                wait_all(bound_back, 3)
                for k in range(1, ns):
                    source = lax.rem(shard - k + ns, ns)
                    for i in range(cap):
                        back[pl.ds(source * cap + i, 1), :] = bound_back[k - 1, pl.ds(i, 1), :]
                wait_all(hub_back, 1)
                back[pl.ds(ns * cap, hubs_own), :] = hub_send[me] + jnp.sum(hub_back[...], axis=0)
                grad_features[...] = grad_features[...] + contract_rows(
                    pick[...].astype(BF), back[...].astype(BF)
                )
    for q in range(pieces):
        finish(flying[q])
        out = grad_self if q // COLUMN_PARTS == 0 else grad_neigh
        out[:, pl.ds((q % COLUMN_PARTS) * part, part)] = gathered[q].astype(F32)


def body(nd, ns, features, w_self, w_neigh, cotangent, neighbours, hub_slots, send_rows, send_counts):
    verts, width = features.shape
    cap = send_rows.shape[2]
    hubs_own = hub_slots.shape[0]
    devices = nd * ns
    extra = round_up(hubs_own * devices + ns * cap, 128)
    picks = round_up(ns * cap + hubs_own, 16)
    pieces = 2 * COLUMN_PARTS
    part = width // COLUMN_PARTS
    plane = (nd // 2) * 2
    tall = ns // 2
    half = width // 2
    rows2 = half // plane
    scatter = rows2 % (tall * ROW_TILE) == 0
    rows3 = rows2 // tall if scatter else rows2
    landings = tall - 1 if scatter else tall
    most = max(plane, tall) - 1
    vmem = pl.BlockSpec(memory_space=pltpu.VMEM)
    smem = pl.BlockSpec(memory_space=pltpu.SMEM)
    return pl.pallas_call(
        functools.partial(kernel, nd, ns),
        out_shape=(
            jax.ShapeDtypeStruct((verts, width), BF),
            jax.ShapeDtypeStruct((verts, width), F32),
            jax.ShapeDtypeStruct((width, width), F32),
            jax.ShapeDtypeStruct((width, width), F32),
        ),
        in_specs=[vmem] * 5 + [smem] * 3,
        out_specs=[vmem] * 4,
        scratch_shapes=[
            pltpu.VMEM((picks, verts), F32),
            pltpu.VMEM((picks, width), F32),
            pltpu.VMEM((hubs_own, width), F32),
            pltpu.VMEM((devices - 1, hubs_own, width), F32),
            pltpu.VMEM((ns, cap, width), F32),
            pltpu.VMEM((ns - 1, cap, width), F32),
            pltpu.VMEM((extra, width), F32),
            pltpu.VMEM((verts, verts + extra), BF),
            pltpu.VMEM((verts, width), BF),
            pltpu.VMEM((verts, width), F32),
            pltpu.VMEM((verts, width), BF),
            pltpu.VMEM((verts, width), BF),
            pltpu.VMEM((extra, width), F32),
            pltpu.VMEM((devices, hubs_own, width), F32),
            pltpu.VMEM((devices - 1, hubs_own, width), F32),
            pltpu.VMEM((ns, cap, width), F32),
            pltpu.VMEM((ns - 1, cap, width), F32),
            pltpu.VMEM((picks, width), F32),
            pltpu.VMEM((pieces, half, part), BF),
            pltpu.VMEM((pieces, half, part), BF),
            pltpu.VMEM((pieces, half, part), F32),
            pltpu.VMEM((pieces, plane - 1, rows2, part), BF),
            pltpu.VMEM((pieces, plane - 1, rows2, part), BF),
            pltpu.VMEM((pieces, rows2, part), F32),
            pltpu.VMEM((pieces, tall - 1, rows3, part), BF),
            pltpu.VMEM((pieces, landings, rows3, part), BF),
            pltpu.VMEM((pieces, width, part), BF),
            pltpu.SemaphoreType.DMA((4,)),
            pltpu.SemaphoreType.DMA((4,)),
            pltpu.SemaphoreType.DMA((pieces, 6, most)),
            pltpu.SemaphoreType.DMA((pieces, 6, most)),
        ],
        compiler_params=pltpu.CompilerParams(
            collective_id=0, has_side_effects=True, vmem_limit_bytes=40 * 1024 * 1024
        ),
    )(features, w_self, w_neigh, cotangent, neighbours, hub_slots, send_rows, send_counts)


def solution(mesh):
    both = ("dom", "shard")
    return jax.shard_map(
        functools.partial(body, mesh.shape["dom"], mesh.shape["shard"]),
        mesh=mesh,
        in_specs=(
            P(both, None),
            P(),
            P(),
            P(both, None),
            P(both, None),
            P(both),
            P(both, None, None),
            P(both, None),
        ),
        out_specs=(P(both, None), P(both, None), P(), P()),
        check_vma=False,
    )
```

time: 186 us -> 48.8 us (0.26)
  blocking collectives: 138 us -> 0 us
  Pallas kernels: 0 us -> 38.1 us
  between operations: 14.9 us -> 1.31 us
  starting transfers between devices: 10.6 us -> 0 us
  matrix products: 9.33 us -> 0 us
  waiting for transfers between devices: 3.83 us -> 0 us
    all_gather x1 -> x0, blocking collectives: 68.1 us -> none  [body(): lax.all_gather(picked[:hubs_own], ('dom', 'shard'), axis=0, tiled=True)]
    unnamed x1 -> x0, blocking collectives: 40.3 us -> none
    pallas_call x0 -> x1, Pallas kernels: none -> 38.1 us  [body(): pl.pallas_call(functools.partial(kernel, nd, ns), out_shape=(jax.ShapeDty...]
    all_to_all x1 -> x0, blocking collectives: 29.3 us -> none  [body(): lax.all_to_all(both.reshape(devices, -1, width), ('dom', 'shard'), split_...]
    all_to_all x2 -> x0, starting transfers between devices: 10.6 us -> none  [the longest x1 7.25 us: body(): lax.all_to_all(outgoing, 'shard', split_axis=0, concat_axis=0, tiled=True)]
    dot_general x9 -> x0, matrix products: 9.33 us -> none  [the longest x4 3.68 us: contract_rows(): lax.dot_general(left, right, (((0,), (0,)), ((), ())), preferred_element_...]
    unnamed x13 -> x16, local copies, waits for them, and re-layouts: 0.89 us -> 9.04 us
    slice x6 -> x0, local copies, waits for them, and re-layouts: 4.83 us -> none  [the longest x1 2.81 us: body(): return (hidden, grad_features, total[:width], total[width:])]
  transfers between devices with their start and end apart: 3 -> 0, of which waited for: 1 -> 0; matrix products, arithmetic and copies ran while one was open for 4% -> 0% of each run, Pallas kernels for 0% -> 0%
where the time goes in v2:
time: 48.8 us; the launch traced here: 48.5 us
  Pallas kernels  38.1 us (78%)
  local copies, waits for them, and re-layouts  9.04 us (19%)
  between operations  1.31 us (3%)
    pallas_call x1, Pallas kernels, body(): pl.pallas_call(functools.partial(kernel, nd, ns), out_shape=(jax.ShapeDty...  38.1 us
    unnamed x16, local copies, waits for them, and re-layouts  9.04 us

profile of v2, /device:TPU:0, one launch (start us, length us, event | category | flops | bytes accessed | tf_op | source)
XLA Modules:
  0.0 48.5 jit_solution(14054943381562902474)
XLA Ops:
  1.3 0.8 %copy.13.send_rows = s32[1,8,4]{2,1,0:T(8,128)S(1)} copy(s32[1,8,4]{1,2,0:T(4,128)} %param.14) | data formatting | bytes 256 | tf_op args[6]
  2.0 0.0 copy-start.4
  2.0 0.9 %copy.12.neighbours = s32[256,32]{1,0:T(8,128)S(1)} copy(s32[256,32]{0,1:T(8,128)} %param.12) | data formatting | bytes 65536 | tf_op args[4]
  2.9 0.0 copy-done.4
  2.9 0.0 copy-start
  2.9 1.0 %copy-done = bf16[512,512]{1,0:T(8,128)(2,1)S(1)} copy-done((bf16[512,512]{1,0:T(8,128)(2,1)S(1)}, bf16[512,512]{1,0:T(8,128)(2,1)}, u32[]{:S(2)}) %copy-start) | copy-done | bytes 524312
  4.0 0.0 copy-start.1
  4.0 1.0 %copy-done.1 = bf16[512,512]{1,0:T(8,128)(2,1)S(1)} copy-done((bf16[512,512]{1,0:T(8,128)(2,1)S(1)}, bf16[512,512]{1,0:T(8,128)(2,1)}, u32[]{:S(2)}) %copy-start.1) | copy-done | bytes 524312
  5.0 0.0 copy-start.2
  5.0 0.9 %copy-done.2 = bf16[256,512]{1,0:T(8,128)(2,1)S(1)} copy-done((bf16[256,512]{1,0:T(8,128)(2,1)S(1)}, bf16[256,512]{1,0:T(8,128)(2,1)}, u32[]{:S(2)}) %copy-start.2) | copy-done | bytes 262168
  6.0 0.0 copy-start.3
  6.0 0.9 %copy-done.3 = bf16[256,512]{1,0:T(8,128)(2,1)S(1)} copy-done((bf16[256,512]{1,0:T(8,128)(2,1)S(1)}, bf16[256,512]{1,0:T(8,128)(2,1)}, u32[]{:S(2)}) %copy-start.3) | copy-done | bytes 262168
  6.9 38.1 %shard_map.111 = (bf16[256,512]{1,0:T(8,128)(2,1)S(1)}, f32[256,512]{1,0:T(8,128)S(1)}, f32[512,512]{1,0:T(8,128)S(1)}, f32[512,512]{1,0:T(8,128)S(1)}) custom-call(bf16[256,512]{1,0:T(8,128)(2,1)S(1)} %copy-done.2, bf16[512,512]{1,0:T(8,128)(2,1)S(1)} %copy-done, bf16[512,512]{1,0:T(8,128)(2,1)S(1)} %copy-done.1, bf16[256,512]{1,0:T(8,128)(2,1)S(1)} %copy-done.3, ...), custom_call_target="tpu_custom_call" | custom-call | tf_op jit(solution)/shard_map/pallas_call | solution.py:361
  45.0 0.7 %copy.19 = bf16[256,512]{1,0:T(8,128)(2,1)} copy(bf16[256,512]{1,0:T(8,128)(2,1)S(1)} %get-tuple-element.8) | data formatting | bytes 524288
  45.7 0.8 %copy.20 = f32[256,512]{1,0:T(8,128)} copy(f32[256,512]{1,0:T(8,128)S(1)} %get-tuple-element.9) | data formatting | bytes 1048576
  46.5 1.0 %copy.21 = f32[512,512]{1,0:T(8,128)} copy(f32[512,512]{1,0:T(8,128)S(1)} %get-tuple-element.10) | data formatting | bytes 2097152
  47.5 1.0 %copy.22 = f32[512,512]{1,0:T(8,128)} copy(f32[512,512]{1,0:T(8,128)S(1)} %get-tuple-element.11) | data formatting | bytes 2097152
Async XLA Ops:
  2.0 0.9 %copy-start.4 = (s32[1,8]{1,0:T(1,128)S(1)}, s32[1,8]{1,0:T(1,128)}, u32[]{:S(2)}) copy-start(s32[1,8]{1,0:T(1,128)} %send_counts.1) | copy-start | bytes 100
  2.9 1.0 %copy-start = (bf16[512,512]{1,0:T(8,128)(2,1)S(1)}, bf16[512,512]{1,0:T(8,128)(2,1)}, u32[]{:S(2)}) copy-start(bf16[512,512]{1,0:T(8,128)(2,1)} %w_self.1) | copy-start | bytes 1572868
  4.0 1.0 %copy-start.1 = (bf16[512,512]{1,0:T(8,128)(2,1)S(1)}, bf16[512,512]{1,0:T(8,128)(2,1)}, u32[]{:S(2)}) copy-start(bf16[512,512]{1,0:T(8,128)(2,1)} %w_neigh.1) | copy-start | bytes 1572868
  5.0 0.9 %copy-start.2 = (bf16[256,512]{1,0:T(8,128)(2,1)S(1)}, bf16[256,512]{1,0:T(8,128)(2,1)}, u32[]{:S(2)}) copy-start(bf16[256,512]{1,0:T(8,128)(2,1)} %features.1) | copy-start | bytes 786436
  6.0 0.9 %copy-start.3 = (bf16[256,512]{1,0:T(8,128)(2,1)S(1)}, bf16[256,512]{1,0:T(8,128)(2,1)}, u32[]{:S(2)}) copy-start(bf16[256,512]{1,0:T(8,128)(2,1)} %cotangent.1) | copy-start | bytes 786436

commit v3 on v2

--- a/solution.py
+++ b/solution.py
@@ -12,6 +12,7 @@
 MESH = pl.DeviceIdType.MESH
 COLUMN_PARTS = 1
 ROW_TILE = 16
+VMEM_GRANT = 60 * 1024 * 1024
 
 
 def contract_rows(left, right):
@@ -32,17 +33,20 @@
 
 def kernel(
     nd, ns,
-    features, w_self, w_neigh, cotangent, neighbours, hub_slots, send_rows, send_counts,
-    hidden, grad_features, grad_self, grad_neigh,
+    features_hbm, w_self_hbm, w_neigh_hbm, cotangent_hbm, neighbours_hbm, rows_hbm, counts_hbm,
+    hub_slots,
+    hidden_hbm, grad_features_hbm, gathered_hbm,
+    hidden, grad_features, store_sems,
+    features, w_self, w_neigh, cotangent, neighbours, send_rows, send_counts, load_sems,
     pick, picked, hub_out, hub_in, bound_out, bound_in, table, count, agg, zs, dz, eg, accum,
     hub_send, hub_back, bound_send, bound_back, back,
     s1, r1, acc1, s2, r2, acc2, s3, r3, gathered,
     small_send, small_recv, send_sems, recv_sems,
 ):
     verts, width = features.shape
-    slots = neighbours.shape[1]
+    slots = neighbours.shape[0]
     devices = nd * ns
-    cap = send_rows.shape[2]
+    cap = send_rows.shape[1]
     hubs_own = hub_slots.shape[0]
     hub_count = hubs_own * devices
     live_rows = hub_count + ns * cap
@@ -58,6 +62,19 @@
     def device_of(index):
         return (lax.div(index, ns), lax.rem(index, ns))
 
+    pairs = (
+        (rows_hbm, send_rows),
+        (counts_hbm, send_counts),
+        (features_hbm, features),
+        (neighbours_hbm, neighbours),
+        (w_self_hbm, w_self),
+        (w_neigh_hbm, w_neigh),
+        (cotangent_hbm, cotangent),
+    )
+    loads = [pltpu.make_async_copy(a, b, load_sems.at[i]) for i, (a, b) in enumerate(pairs)]
+    for load in loads:
+        load.start()
+
     barrier = pltpu.get_barrier_semaphore()
 
     def greet(k, carry):
@@ -70,12 +87,15 @@
 
     lane = lax.broadcasted_iota(jnp.int32, (1, verts), 1)
     pick[...] = jnp.zeros_like(pick)
+    loads[0].wait()
+    loads[1].wait()
     for p in range(ns):
         for k in range(cap):
-            row = jnp.where(k < send_counts[0, p], send_rows[0, p, k], -1)
+            row = jnp.where(k < send_counts[0, p], send_rows[0, k, p], -1)
             pick[pl.ds(p * cap + k, 1), :] = (lane == row).astype(F32)
     for h in range(hubs_own):
         pick[pl.ds(ns * cap + h, 1), :] = (lane == hub_slots[h]).astype(F32)
+    loads[2].wait()
     picked[...] = dot(pick[...].astype(BF), features[...])
     for p in range(ns):
         bound_out[p] = picked[pl.ds(p * cap, cap), :]
@@ -132,23 +152,25 @@
     start_all(bound_copy(bound_out, bound_in, 2), ns)
     start_all(hub_copy, devices)
 
-    block = 32
-    columns = count.shape[1]
-    names = lax.broadcasted_iota(jnp.int32, (block, columns), 1)
+    block = 64
+    names = lax.broadcasted_iota(jnp.int32, (block, verts), 0)
+    loads[3].wait()
 
     def count_block(i, carry):
-        rows = pl.ds(pl.multiple_of(i * block, block), block)
-        slot = neighbours[rows, :]
-        total = jnp.zeros((block, columns), F32)
+        first = pl.multiple_of(i * block, block)
+        total = jnp.zeros((block, verts), F32)
         for j in range(slots):
-            total = total + (slot[:, j : j + 1] == names).astype(F32)
-        count[rows, :] = total.astype(BF)
+            total = total + (neighbours[pl.ds(j, 1), :] - first == names).astype(F32)
+        count[pl.ds(first, block), :] = total.astype(BF)
         return carry
 
-    lax.fori_loop(0, verts // block, count_block, 0)
-    degree = jnp.sum((neighbours[...] < table_size).astype(F32), axis=1, keepdims=True)
+    lax.fori_loop(0, count.shape[0] // block, count_block, 0)
+    alive = (neighbours[...] < table_size).astype(F32).astype(BF)
+    degree = contract_rows(alive, jnp.ones((slots, 128), BF))
+    degree = jnp.concatenate([degree] * (width // 128), axis=1)
+    loads[4].wait()
     zs[...] = dot(features[...], w_self[...])
-    local_sums = dot(count[:, :verts], features[...])
+    local_sums = contract_rows(count[:verts, :], features[...])
 
     table[...] = jnp.zeros_like(table)
     for h in range(hubs_own):
@@ -170,11 +192,15 @@
 
     lax.fori_loop(1, devices, place_hub, 0)
 
-    sums = local_sums + dot(count[:, verts:], table[...].astype(BF))
+    loads[5].wait()
+    loads[6].wait()
+    sums = local_sums + contract_rows(count[verts:, :], table[...].astype(BF))
     agg[...] = (sums / degree).astype(BF)
     z = zs[...] + dot(agg[...], w_neigh[...])
     sig = jax.nn.sigmoid(z)
     hidden[...] = (z * sig).astype(BF)
+    stores = [pltpu.make_async_copy(hidden, hidden_hbm, store_sems.at[0])]
+    stores[0].start()
     dz[...] = (cotangent[...].astype(F32) * sig * (1.0 + z * (1.0 - sig))).astype(BF)
 
     part = width // COLUMN_PARTS
@@ -303,7 +329,7 @@
             flying[q] = stages[number](q)
             if number == 1 and q == 0:
                 eg[...] = (contract_cols(dz[...], w_neigh[...]) / degree).astype(BF)
-                accum[...] = contract_rows(count[:, verts:], eg[...])
+                accum[...] = dot(count[verts:, :], eg[...])
 
                 def fill(d, carry):
                     for h in range(hubs_own):
@@ -316,8 +342,8 @@
                 start_all(bound_copy(bound_send, bound_back, 3), ns)
                 start_all(hub_return, devices)
             if number == 2 and q == 0:
-                grad_features[...] = contract_cols(dz[...], w_self[...]) + contract_rows(
-                    count[:, :verts], eg[...]
+                grad_features[...] = contract_cols(dz[...], w_self[...]) + dot(
+                    count[:verts, :], eg[...]
                 )
             if number == 4 and q == pieces - 1:
                 back[...] = jnp.zeros_like(back)
@@ -333,10 +359,53 @@
                 grad_features[...] = grad_features[...] + contract_rows(
                     pick[...].astype(BF), back[...].astype(BF)
                 )
+                stores.append(
+                    pltpu.make_async_copy(grad_features, grad_features_hbm, store_sems.at[1])
+                )
+                stores[-1].start()
     for q in range(pieces):
         finish(flying[q])
+        stores.append(
+            pltpu.make_async_copy(gathered.at[q], gathered_hbm.at[q], store_sems.at[2 + q])
+        )
+        stores[-1].start()
+    for store in stores:
+        store.wait()
+
+
+def writer(
+    hidden_in, grad_features_in, gathered_in, hidden, grad_features, grad_self, grad_neigh,
+    narrow, wide, in_sems, out_sems,
+):
+    pieces, width, part = narrow.shape
+    cuts = in_sems.shape[1]
+    step = width // cuts
+    places = [(q, i) for q in range(pieces) for i in range(cuts)]
+    reads = []
+    for q, i in places:
+        rows = pl.ds(i * step, step)
+        reads.append(
+            pltpu.make_async_copy(gathered_in.at[q, rows], narrow.at[q, rows], in_sems.at[q, i])
+        )
+        reads[-1].start()
+    writes = [
+        pltpu.make_async_copy(hidden_in, hidden, out_sems.at[pieces, 0]),
+        pltpu.make_async_copy(grad_features_in, grad_features, out_sems.at[pieces, 1]),
+    ]
+    for c in writes:
+        c.start()
+    for read, (q, i) in zip(reads, places):
+        read.wait()
+        rows = pl.ds(i * step, step)
+        cols = pl.ds((q % COLUMN_PARTS) * part, part)
+        wide[q, rows, :] = narrow[q, rows, :].astype(F32)
         out = grad_self if q // COLUMN_PARTS == 0 else grad_neigh
-        out[:, pl.ds((q % COLUMN_PARTS) * part, part)] = gathered[q].astype(F32)
+        writes.append(
+            pltpu.make_async_copy(wide.at[q, rows], out.at[rows, cols], out_sems.at[q, i])
+        )
+        writes[-1].start()
+    for c in writes:
+        c.wait()
 
 
 def body(nd, ns, features, w_self, w_neigh, cotangent, neighbours, hub_slots, send_rows, send_counts):
@@ -356,19 +425,31 @@
     rows3 = rows2 // tall if scatter else rows2
     landings = tall - 1 if scatter else tall
     most = max(plane, tall) - 1
-    vmem = pl.BlockSpec(memory_space=pltpu.VMEM)
     smem = pl.BlockSpec(memory_space=pltpu.SMEM)
-    return pl.pallas_call(
+    hbm = pl.BlockSpec(memory_space=pltpu.HBM)
+    shapes = (
+        jax.ShapeDtypeStruct((verts, width), BF),
+        jax.ShapeDtypeStruct((verts, width), F32),
+        jax.ShapeDtypeStruct((width, width), F32),
+        jax.ShapeDtypeStruct((width, width), F32),
+    )
+    results = pl.pallas_call(
         functools.partial(kernel, nd, ns),
-        out_shape=(
-            jax.ShapeDtypeStruct((verts, width), BF),
-            jax.ShapeDtypeStruct((verts, width), F32),
-            jax.ShapeDtypeStruct((width, width), F32),
-            jax.ShapeDtypeStruct((width, width), F32),
-        ),
-        in_specs=[vmem] * 5 + [smem] * 3,
-        out_specs=[vmem] * 4,
+        out_shape=shapes[:2] + (jax.ShapeDtypeStruct((pieces, width, part), BF),),
+        in_specs=[hbm] * 7 + [smem],
+        out_specs=[hbm] * 3,
         scratch_shapes=[
+            pltpu.VMEM((verts, width), BF),
+            pltpu.VMEM((verts, width), F32),
+            pltpu.SemaphoreType.DMA((2 + pieces,)),
+            pltpu.VMEM((verts, width), BF),
+            pltpu.VMEM((width, width), BF),
+            pltpu.VMEM((width, width), BF),
+            pltpu.VMEM((verts, width), BF),
+            pltpu.VMEM((neighbours.shape[1], verts), jnp.int32),
+            pltpu.SMEM((1, cap, ns), jnp.int32),
+            pltpu.SMEM((1, ns), jnp.int32),
+            pltpu.SemaphoreType.DMA((7,)),
             pltpu.VMEM((picks, verts), F32),
             pltpu.VMEM((picks, width), F32),
             pltpu.VMEM((hubs_own, width), F32),
@@ -376,7 +457,7 @@
             pltpu.VMEM((ns, cap, width), F32),
             pltpu.VMEM((ns - 1, cap, width), F32),
             pltpu.VMEM((extra, width), F32),
-            pltpu.VMEM((verts, verts + extra), BF),
+            pltpu.VMEM((verts + extra, verts), BF),
             pltpu.VMEM((verts, width), BF),
             pltpu.VMEM((verts, width), F32),
             pltpu.VMEM((verts, width), BF),
@@ -402,9 +483,25 @@
             pltpu.SemaphoreType.DMA((pieces, 6, most)),
         ],
         compiler_params=pltpu.CompilerParams(
-            collective_id=0, has_side_effects=True, vmem_limit_bytes=40 * 1024 * 1024
+            collective_id=0, has_side_effects=True, vmem_limit_bytes=VMEM_GRANT
         ),
-    )(features, w_self, w_neigh, cotangent, neighbours, hub_slots, send_rows, send_counts)
+    )(
+        features, w_self, w_neigh, cotangent, neighbours.T, send_rows.transpose(0, 2, 1),
+        send_counts, hub_slots,
+    )
+    return pl.pallas_call(
+        writer,
+        out_shape=shapes,
+        in_specs=[hbm] * 3,
+        out_specs=[hbm] * 4,
+        scratch_shapes=[
+            pltpu.VMEM((pieces, width, part), BF),
+            pltpu.VMEM((pieces, width, part), F32),
+            pltpu.SemaphoreType.DMA((pieces, 2)),
+            pltpu.SemaphoreType.DMA((pieces + 1, 2)),
+        ],
+        compiler_params=pltpu.CompilerParams(vmem_limit_bytes=VMEM_GRANT),
+    )(*results)
 
 
 def solution(mesh):

time: 48.8 us -> 64.9 us (1.33)
  Pallas kernels: 38.1 us -> 63.4 us
  local copies, waits for them, and re-layouts: 9.04 us -> 0 us
    pallas_call x1 -> x2, Pallas kernels: 38.1 us -> 63.4 us  [the longest x1 38.4 us: body(): pl.pallas_call(functools.partial(kernel, nd, ns), out_shape=shapes[:2] +...]
    unnamed x16 -> x0, local copies, waits for them, and re-layouts: 9.04 us -> none
where the time goes in v3:
time: 64.9 us; the launch traced here: 64.7 us
  Pallas kernels  63.4 us (98%)
  between operations  1.29 us (2%)
    pallas_call x1, Pallas kernels, body(): pl.pallas_call(functools.partial(kernel, nd, ns), out_shape=shapes[:2] +...  38.4 us
    pallas_call x1, Pallas kernels, body(): pl.pallas_call(writer, out_shape=shapes, in_specs=[hbm] * 3, out_specs=[h...  25 us

profile of v3, /device:TPU:0, one launch (start us, length us, event | category | flops | bytes accessed | tf_op | source)
XLA Modules:
  0.0 64.7 jit_solution(2508205547518548347)
XLA Ops:
  1.3 38.4 %shard_map.111 = (bf16[256,512]{1,0:T(8,128)(2,1)}, f32[256,512]{1,0:T(8,128)}, bf16[2,512,512]{2,1,0:T(8,128)(2,1)}) custom-call(bf16[256,512]{1,0:T(8,128)(2,1)} %features_hbm.1, bf16[512,512]{1,0:T(8,128)(2,1)} %w_self_hbm.1, bf16[512,512]{1,0:T(8,128)(2,1)} %w_neigh_hbm.1, bf16[256,512]{1,0:T(8,128)(2,1)} %cotangent_hbm.1, s32[32,256]{1,0:T(8,128)} %bitcast.2, ...), custom_call_target="tpu_custom_call" | custom-call | tf_op jit(solution)/shard_map/pallas_call | solution.py:436
  39.7 25.0 %shard_map.112 = (bf16[256,512]{1,0:T(8,128)(2,1)}, f32[256,512]{1,0:T(8,128)}, f32[512,512]{1,0:T(8,128)}, f32[512,512]{1,0:T(8,128)}) custom-call(bf16[256,512]{1,0:T(8,128)(2,1)} %get-tuple-element.7.hidden_in, f32[256,512]{1,0:T(8,128)} %get-tuple-element.8.grad_features_in, bf16[2,512,512]{2,1,0:T(8,128)(2,1)} %get-tuple-element.9.gathered_in), custom_call_target="tpu_custom_call" | custom-call | tf_op jit(solution)/shard_map/pallas_call | solution.py:492

commit v4 on v3

--- a/solution.py
+++ b/solution.py
@@ -375,12 +375,19 @@
 
 def writer(
     hidden_in, grad_features_in, gathered_in, hidden, grad_features, grad_self, grad_neigh,
-    narrow, wide, in_sems, out_sems,
+    narrow, wide, hidden_held, grad_held, in_sems, out_sems,
 ):
     pieces, width, part = narrow.shape
     cuts = in_sems.shape[1]
     step = width // cuts
     places = [(q, i) for q in range(pieces) for i in range(cuts)]
+    passed = (
+        (hidden_in, hidden_held, hidden),
+        (grad_features_in, grad_held, grad_features),
+    )
+    writes = []
+    for i, (a, b, c) in enumerate(passed):
+        pltpu.make_async_copy(a, b, in_sems.at[pieces, i]).start()
     reads = []
     for q, i in places:
         rows = pl.ds(i * step, step)
@@ -388,12 +395,10 @@
             pltpu.make_async_copy(gathered_in.at[q, rows], narrow.at[q, rows], in_sems.at[q, i])
         )
         reads[-1].start()
-    writes = [
-        pltpu.make_async_copy(hidden_in, hidden, out_sems.at[pieces, 0]),
-        pltpu.make_async_copy(grad_features_in, grad_features, out_sems.at[pieces, 1]),
-    ]
-    for c in writes:
-        c.start()
+    for i, (a, b, c) in enumerate(passed):
+        pltpu.make_async_copy(a, b, in_sems.at[pieces, i]).wait()
+        writes.append(pltpu.make_async_copy(b, c, out_sems.at[pieces, i]))
+        writes[-1].start()
     for read, (q, i) in zip(reads, places):
         read.wait()
         rows = pl.ds(i * step, step)
@@ -497,7 +502,9 @@
         scratch_shapes=[
             pltpu.VMEM((pieces, width, part), BF),
             pltpu.VMEM((pieces, width, part), F32),
-            pltpu.SemaphoreType.DMA((pieces, 2)),
+            pltpu.VMEM((verts, width), BF),
+            pltpu.VMEM((verts, width), F32),
+            pltpu.SemaphoreType.DMA((pieces + 1, 2)),
             pltpu.SemaphoreType.DMA((pieces + 1, 2)),
         ],
         compiler_params=pltpu.CompilerParams(vmem_limit_bytes=VMEM_GRANT),

time: 64.9 us -> 42.6 us (0.66)
  Pallas kernels: 63.4 us -> 41.1 us
    pallas_call x1, Pallas kernels: 25 us -> 2.71 us  [body(): pl.pallas_call(writer, out_shape=shapes, in_specs=[hbm] * 3, out_specs=[h...]
where the time goes in v4:
time: 42.6 us; the launch traced here: 42.4 us
  Pallas kernels  41.1 us (96%)
  between operations  1.29 us (3%)
    pallas_call x1, Pallas kernels, body(): pl.pallas_call(functools.partial(kernel, nd, ns), out_shape=shapes[:2] +...  38.4 us
    pallas_call x1, Pallas kernels, body(): pl.pallas_call(writer, out_shape=shapes, in_specs=[hbm] * 3, out_specs=[h...  2.71 us

profile of v4, /device:TPU:0, one launch (start us, length us, event | category | flops | bytes accessed | tf_op | source)
XLA Modules:
  0.0 42.4 jit_solution(15197783191483370353)
XLA Ops:
  1.3 38.4 %shard_map.111 = (bf16[256,512]{1,0:T(8,128)(2,1)}, f32[256,512]{1,0:T(8,128)}, bf16[2,512,512]{2,1,0:T(8,128)(2,1)}) custom-call(bf16[256,512]{1,0:T(8,128)(2,1)} %features_hbm.1, bf16[512,512]{1,0:T(8,128)(2,1)} %w_self_hbm.1, bf16[512,512]{1,0:T(8,128)(2,1)} %w_neigh_hbm.1, bf16[256,512]{1,0:T(8,128)(2,1)} %cotangent_hbm.1, s32[32,256]{1,0:T(8,128)} %bitcast.2, ...), custom_call_target="tpu_custom_call" | custom-call | tf_op jit(solution)/shard_map/pallas_call | solution.py:441
  39.7 2.7 %shard_map.112 = (bf16[256,512]{1,0:T(8,128)(2,1)}, f32[256,512]{1,0:T(8,128)}, f32[512,512]{1,0:T(8,128)}, f32[512,512]{1,0:T(8,128)}) custom-call(bf16[256,512]{1,0:T(8,128)(2,1)} %get-tuple-element.7.hidden_in, f32[256,512]{1,0:T(8,128)} %get-tuple-element.8.grad_features_in, bf16[2,512,512]{2,1,0:T(8,128)(2,1)} %get-tuple-element.9.gathered_in), custom_call_target="tpu_custom_call" | custom-call | tf_op jit(solution)/shard_map/pallas_call | solution.py:497

commit v5 on v4

--- a/solution.py
+++ b/solution.py
@@ -10,7 +10,7 @@
 BF = jnp.bfloat16
 F32 = jnp.float32
 MESH = pl.DeviceIdType.MESH
-COLUMN_PARTS = 1
+COLUMN_PARTS = 2
 ROW_TILE = 16
 VMEM_GRANT = 60 * 1024 * 1024
 
@@ -322,12 +322,14 @@
             c.wait()
 
     stages = [stage0, stage1, stage2, stage3, stage4, stage5]
-    flying = [stage0(q) for q in range(pieces)]
+    flying = [stage0(0)]
     for number in range(1, len(stages)):
         for q in range(pieces):
+            if number == 1 and q + 1 < pieces:
+                flying.append(stage0(q + 1))
             finish(flying[q])
             flying[q] = stages[number](q)
-            if number == 1 and q == 0:
+            if number == 1 and q == pieces - 1:
                 eg[...] = (contract_cols(dz[...], w_neigh[...]) / degree).astype(BF)
                 accum[...] = dot(count[verts:, :], eg[...])
 
@@ -341,7 +343,6 @@
                     bound_send[p] = accum[pl.ds(hub_count + p * cap, cap), :]
                 start_all(bound_copy(bound_send, bound_back, 3), ns)
                 start_all(hub_return, devices)
-            if number == 2 and q == 0:
                 grad_features[...] = contract_cols(dz[...], w_self[...]) + dot(
                     count[:verts, :], eg[...]
                 )

time: 42.6 us -> 41.6 us (0.977)
  Pallas kernels: 41.1 us -> 40.1 us
    pallas_call x1, Pallas kernels: 38.4 us -> 37.4 us  [body(): pl.pallas_call(functools.partial(kernel, nd, ns), out_shape=shapes[:2] +...]
where the time goes in v5:
time: 41.6 us; the launch traced here: 41.4 us
  Pallas kernels  40.1 us (96%)
  between operations  1.29 us (3%)
    pallas_call x1, Pallas kernels, body(): pl.pallas_call(functools.partial(kernel, nd, ns), out_shape=shapes[:2] +...  37.4 us
    pallas_call x1, Pallas kernels, body(): pl.pallas_call(writer, out_shape=shapes, in_specs=[hbm] * 3, out_specs=[h...  2.78 us

profile of v5, /device:TPU:0, one launch (start us, length us, event | category | flops | bytes accessed | tf_op | source)
XLA Modules:
  0.0 41.4 jit_solution(12132272608017313564)
XLA Ops:
  1.3 37.4 %shard_map.111 = (bf16[256,512]{1,0:T(8,128)(2,1)}, f32[256,512]{1,0:T(8,128)}, bf16[4,512,256]{2,1,0:T(8,128)(2,1)}) custom-call(bf16[256,512]{1,0:T(8,128)(2,1)} %features_hbm.1, bf16[512,512]{1,0:T(8,128)(2,1)} %w_self_hbm.1, bf16[512,512]{1,0:T(8,128)(2,1)} %w_neigh_hbm.1, bf16[256,512]{1,0:T(8,128)(2,1)} %cotangent_hbm.1, s32[32,256]{1,0:T(8,128)} %bitcast.2, ...), custom_call_target="tpu_custom_call" | custom-call | tf_op jit(solution)/shard_map/pallas_call | solution.py:442
  38.7 2.8 %shard_map.112 = (bf16[256,512]{1,0:T(8,128)(2,1)}, f32[256,512]{1,0:T(8,128)}, f32[512,512]{1,0:T(8,128)}, f32[512,512]{1,0:T(8,128)}) custom-call(bf16[256,512]{1,0:T(8,128)(2,1)} %get-tuple-element.7.hidden_in, f32[256,512]{1,0:T(8,128)} %get-tuple-element.8.grad_features_in, bf16[4,512,256]{2,1,0:T(8,128)(2,1)} %get-tuple-element.9.gathered_in), custom_call_target="tpu_custom_call" | custom-call | tf_op jit(solution)/shard_map/pallas_call | solution.py:498

commit v6 on v5

--- a/solution.py
+++ b/solution.py
@@ -36,7 +36,7 @@
     features_hbm, w_self_hbm, w_neigh_hbm, cotangent_hbm, neighbours_hbm, rows_hbm, counts_hbm,
     hub_slots,
     hidden_hbm, grad_features_hbm, gathered_hbm,
-    hidden, grad_features, store_sems,
+    hidden, grad_features, features_t, store_sems,
     features, w_self, w_neigh, cotangent, neighbours, send_rows, send_counts, load_sems,
     pick, picked, hub_out, hub_in, bound_out, bound_in, table, count, agg, zs, dz, eg, accum,
     hub_send, hub_back, bound_send, bound_back, back,
@@ -167,7 +167,8 @@
     lax.fori_loop(0, count.shape[0] // block, count_block, 0)
     alive = (neighbours[...] < table_size).astype(F32).astype(BF)
     degree = contract_rows(alive, jnp.ones((slots, 128), BF))
-    degree = jnp.concatenate([degree] * (width // 128), axis=1)
+    inverse = jnp.concatenate([1.0 / degree] * (width // 128), axis=1)
+    features_t[...] = features[...].T
     loads[4].wait()
     zs[...] = dot(features[...], w_self[...])
     local_sums = contract_rows(count[:verts, :], features[...])
@@ -195,7 +196,7 @@
     loads[5].wait()
     loads[6].wait()
     sums = local_sums + contract_rows(count[verts:, :], table[...].astype(BF))
-    agg[...] = (sums / degree).astype(BF)
+    agg[...] = (sums * inverse).astype(BF)
     z = zs[...] + dot(agg[...], w_neigh[...])
     sig = jax.nn.sigmoid(z)
     hidden[...] = (z * sig).astype(BF)
@@ -213,8 +214,6 @@
     rows3 = rows2 // tall if scatter else rows2
     my_plane = y * 2 + low
     base1 = core * half
-    base2 = base1 + my_plane * rows2
-    base3 = base2 + high * rows3 if scatter else base2
 
     def at_core(j):
         return (y * 2 + j, shard)
@@ -224,6 +223,18 @@
 
     def at_tall(j):
         return (dom, j * 2 + low)
+
+    def route(q):
+        first, second = (plane, my_plane, at_plane), (tall, high, at_tall)
+        if plane == tall and q == pieces // 2 and pieces > 2:
+            return second, first
+        return first, second
+
+    def base2(q):
+        return base1 + route(q)[0][1] * rows2
+
+    def base3(q):
+        return base2(q) + route(q)[1][1] * rows3 if scatter else base2(q)
 
     def copy(q, stage, k, source, landing, target):
         return pltpu.make_async_remote_copy(
@@ -238,75 +249,84 @@
     def rows_at(start, size):
         return pl.ds(pl.multiple_of(start, ROW_TILE), size)
 
-    def left_of(q):
-        return features if q // COLUMN_PARTS == 0 else agg
-
     def right_of(q):
         return dz[:, pl.ds((q % COLUMN_PARTS) * part, part)]
 
     def stage0(q):
         other = pl.ds(pl.multiple_of((1 - core) * half, half), half)
         own = pl.ds(pl.multiple_of(core * half, half), half)
-        s1[q] = contract_rows(left_of(q)[:, other], right_of(q)).astype(BF)
+        turned = q // COLUMN_PARTS == 0
+
+        def product(rows):
+            if turned:
+                return dot(features_t[rows, :], right_of(q))
+            return contract_rows(agg[:, rows], right_of(q))
+
+        s1[q] = product(other).astype(BF)
         c = copy(q, 0, 1, s1.at[q], r1.at[q], at_core(1 - core))
         c.start()
-        acc1[q] = contract_rows(left_of(q)[:, own], right_of(q))
+        acc1[q] = product(own)
         return [c]
 
     def stage1(q):
+        size, mine, at = route(q)[0]
         acc1[q] = acc1[q] + r1[q].astype(F32)
         copies = []
-        for k in range(1, plane):
-            j = lax.rem(my_plane + k, plane)
+        for k in range(1, size):
+            j = lax.rem(mine + k, size)
             s2[q, k - 1] = acc1[q, rows_at(j * rows2, rows2), :].astype(BF)
-            c = copy(q, 1, k, s2.at[q, k - 1], r2.at[q, k - 1], at_plane(j))
+            c = copy(q, 1, k, s2.at[q, k - 1], r2.at[q, k - 1], at(j))
             c.start()
             copies.append(c)
         return copies
 
     def stage2(q):
-        total = acc1[q, rows_at(my_plane * rows2, rows2), :]
-        for k in range(1, plane):
+        before, mine, _ = route(q)[0]
+        total = acc1[q, rows_at(mine * rows2, rows2), :]
+        for k in range(1, before):
             total = total + r2[q, k - 1].astype(F32)
         acc2[q] = total
+        size, mine, at = route(q)[1]
         copies = []
         if not scatter:
-            r3[q, high] = total.astype(BF)
-        for k in range(1, tall):
-            j = lax.rem(high + k, tall)
+            r3[q, mine] = total.astype(BF)
+        for k in range(1, size):
+            j = lax.rem(mine + k, size)
             if scatter:
                 s3[q, k - 1] = acc2[q, rows_at(j * rows3, rows3), :].astype(BF)
-                c = copy(q, 2, k, s3.at[q, k - 1], r3.at[q, k - 1], at_tall(j))
+                c = copy(q, 2, k, s3.at[q, k - 1], r3.at[q, k - 1], at(j))
             else:
-                c = copy(q, 2, k, r3.at[q, high], r3.at[q, high], at_tall(j))
+                c = copy(q, 2, k, r3.at[q, mine], r3.at[q, mine], at(j))
             c.start()
             copies.append(c)
         return copies
 
     def stage3(q):
+        size, mine, at = route(q)[1]
         if scatter:
-            total = acc2[q, rows_at(high * rows3, rows3), :]
-            for k in range(1, tall):
+            total = acc2[q, rows_at(mine * rows3, rows3), :]
+            for k in range(1, size):
                 total = total + r3[q, k - 1].astype(F32)
         else:
             total = r3[q, 0].astype(F32)
-            for j in range(1, tall):
+            for j in range(1, size):
                 total = total + r3[q, j].astype(F32)
-        gathered[q, rows_at(base3, rows3), :] = total.astype(BF)
+        gathered[q, rows_at(base3(q), rows3), :] = total.astype(BF)
         copies = []
         if scatter:
-            chunk = gathered.at[q, rows_at(base3, rows3), :]
-            for k in range(1, tall):
-                c = copy(q, 3, k, chunk, chunk, at_tall(lax.rem(high + k, tall)))
+            chunk = gathered.at[q, rows_at(base3(q), rows3), :]
+            for k in range(1, size):
+                c = copy(q, 3, k, chunk, chunk, at(lax.rem(mine + k, size)))
                 c.start()
                 copies.append(c)
         return copies
 
     def stage4(q):
-        chunk = gathered.at[q, rows_at(base2, rows2), :]
+        size, mine, at = route(q)[0]
+        chunk = gathered.at[q, rows_at(base2(q), rows2), :]
         copies = []
-        for k in range(1, plane):
-            c = copy(q, 4, k, chunk, chunk, at_plane(lax.rem(my_plane + k, plane)))
+        for k in range(1, size):
+            c = copy(q, 4, k, chunk, chunk, at(lax.rem(mine + k, size)))
             c.start()
             copies.append(c)
         return copies
@@ -330,7 +350,7 @@
             finish(flying[q])
             flying[q] = stages[number](q)
             if number == 1 and q == pieces - 1:
-                eg[...] = (contract_cols(dz[...], w_neigh[...]) / degree).astype(BF)
+                eg[...] = (contract_cols(dz[...], w_neigh[...]) * inverse).astype(BF)
                 accum[...] = dot(count[verts:, :], eg[...])
 
                 def fill(d, carry):
@@ -447,6 +467,7 @@
         scratch_shapes=[
             pltpu.VMEM((verts, width), BF),
             pltpu.VMEM((verts, width), F32),
+            pltpu.VMEM((width, verts), BF),
             pltpu.SemaphoreType.DMA((2 + pieces,)),
             pltpu.VMEM((verts, width), BF),
             pltpu.VMEM((width, width), BF),

time: 41.6 us -> 41.1 us (0.988)
  Pallas kernels: 40.1 us -> 39.6 us
    pallas_call x1, Pallas kernels: 37.4 us -> 36.8 us  [body(): pl.pallas_call(functools.partial(kernel, nd, ns), out_shape=shapes[:2] +...]
where the time goes in v6:
time: 41.1 us; the launch traced here: 40.9 us
  Pallas kernels  39.6 us (96%)
  between operations  1.29 us (3%)
    pallas_call x1, Pallas kernels, body(): pl.pallas_call(functools.partial(kernel, nd, ns), out_shape=shapes[:2] +...  36.8 us
    pallas_call x1, Pallas kernels, body(): pl.pallas_call(writer, out_shape=shapes, in_specs=[hbm] * 3, out_specs=[h...  2.78 us

profile of v6, /device:TPU:0, one launch (start us, length us, event | category | flops | bytes accessed | tf_op | source)
XLA Modules:
  0.0 40.9 jit_solution(2284854210263358794)
XLA Ops:
  1.3 36.8 %shard_map.111 = (bf16[256,512]{1,0:T(8,128)(2,1)}, f32[256,512]{1,0:T(8,128)}, bf16[4,512,256]{2,1,0:T(8,128)(2,1)}) custom-call(bf16[256,512]{1,0:T(8,128)(2,1)} %features_hbm.1, bf16[512,512]{1,0:T(8,128)(2,1)} %w_self_hbm.1, bf16[512,512]{1,0:T(8,128)(2,1)} %w_neigh_hbm.1, bf16[256,512]{1,0:T(8,128)(2,1)} %cotangent_hbm.1, s32[32,256]{1,0:T(8,128)} %bitcast.2, ...), custom_call_target="tpu_custom_call" | custom-call | tf_op jit(solution)/shard_map/pallas_call | solution.py:462
  38.1 2.8 %shard_map.112 = (bf16[256,512]{1,0:T(8,128)(2,1)}, f32[256,512]{1,0:T(8,128)}, f32[512,512]{1,0:T(8,128)}, f32[512,512]{1,0:T(8,128)}) custom-call(bf16[256,512]{1,0:T(8,128)(2,1)} %get-tuple-element.7.hidden_in, f32[256,512]{1,0:T(8,128)} %get-tuple-element.8.grad_features_in, bf16[4,512,256]{2,1,0:T(8,128)(2,1)} %get-tuple-element.9.gathered_in), custom_call_target="tpu_custom_call" | custom-call | tf_op jit(solution)/shard_map/pallas_call | solution.py:519

commit v7 on v6

--- a/solution.py
+++ b/solution.py
@@ -342,48 +342,59 @@
             c.wait()
 
     stages = [stage0, stage1, stage2, stage3, stage4, stage5]
+    def edge_gradients():
+        eg[...] = (contract_cols(dz[...], w_neigh[...]) * inverse).astype(BF)
+        accum[...] = dot(count[verts:, :], eg[...])
+
+    def send_gradients():
+        def fill(d, carry):
+            for h in range(hubs_own):
+                hub_send[d, pl.ds(h, 1), :] = accum[pl.ds(d * hubs_own + h, 1), :]
+            return carry
+
+        lax.fori_loop(0, devices, fill, 0)
+        for p in range(ns):
+            bound_send[p] = accum[pl.ds(hub_count + p * cap, cap), :]
+        start_all(bound_copy(bound_send, bound_back, 3), ns)
+        start_all(hub_return, devices)
+
+    def own_gradients():
+        grad_features[...] = contract_cols(dz[...], w_self[...]) + dot(count[:verts, :], eg[...])
+
+    def take_gradients():
+        back[...] = jnp.zeros_like(back)
+        for i in range(cap):
+            back[pl.ds(shard * cap + i, 1), :] = bound_send[shard, pl.ds(i, 1), :]
+        wait_all(bound_back, 3)
+        for k in range(1, ns):
+            source = lax.rem(shard - k + ns, ns)
+            for i in range(cap):
+                back[pl.ds(source * cap + i, 1), :] = bound_back[k - 1, pl.ds(i, 1), :]
+        wait_all(hub_back, 1)
+        back[pl.ds(ns * cap, hubs_own), :] = hub_send[me] + jnp.sum(hub_back[...], axis=0)
+        grad_features[...] = grad_features[...] + contract_rows(
+            pick[...].astype(BF), back[...].astype(BF)
+        )
+        stores.append(pltpu.make_async_copy(grad_features, grad_features_hbm, store_sems.at[1]))
+        stores[-1].start()
+
     flying = [stage0(0)]
-    for number in range(1, len(stages)):
-        for q in range(pieces):
-            if number == 1 and q + 1 < pieces:
-                flying.append(stage0(q + 1))
-            finish(flying[q])
-            flying[q] = stages[number](q)
-            if number == 1 and q == pieces - 1:
-                eg[...] = (contract_cols(dz[...], w_neigh[...]) * inverse).astype(BF)
-                accum[...] = dot(count[verts:, :], eg[...])
-
-                def fill(d, carry):
-                    for h in range(hubs_own):
-                        hub_send[d, pl.ds(h, 1), :] = accum[pl.ds(d * hubs_own + h, 1), :]
-                    return carry
-
-                lax.fori_loop(0, devices, fill, 0)
-                for p in range(ns):
-                    bound_send[p] = accum[pl.ds(hub_count + p * cap, cap), :]
-                start_all(bound_copy(bound_send, bound_back, 3), ns)
-                start_all(hub_return, devices)
-                grad_features[...] = contract_cols(dz[...], w_self[...]) + dot(
-                    count[:verts, :], eg[...]
-                )
-            if number == 4 and q == pieces - 1:
-                back[...] = jnp.zeros_like(back)
-                for i in range(cap):
-                    back[pl.ds(shard * cap + i, 1), :] = bound_send[shard, pl.ds(i, 1), :]
-                wait_all(bound_back, 3)
-                for k in range(1, ns):
-                    source = lax.rem(shard - k + ns, ns)
-                    for i in range(cap):
-                        back[pl.ds(source * cap + i, 1), :] = bound_back[k - 1, pl.ds(i, 1), :]
-                wait_all(hub_back, 1)
-                back[pl.ds(ns * cap, hubs_own), :] = hub_send[me] + jnp.sum(hub_back[...], axis=0)
-                grad_features[...] = grad_features[...] + contract_rows(
-                    pick[...].astype(BF), back[...].astype(BF)
-                )
-                stores.append(
-                    pltpu.make_async_copy(grad_features, grad_features_hbm, store_sems.at[1])
-                )
-                stores[-1].start()
+    for q in range(pieces):
+        if q + 1 < pieces:
+            flying.append(stage0(q + 1))
+        finish(flying[q])
+        flying[q] = stage1(q)
+    edge_gradients()
+    steps = [(8 * number + 5 * q, number, q) for number in range(2, 6) for q in range(pieces)]
+    for _, number, q in sorted(steps):
+        finish(flying[q])
+        flying[q] = stages[number](q)
+        if (number, q) == (2, 1):
+            send_gradients()
+        if (number, q) == (2, pieces - 1):
+            own_gradients()
+        if (number, q) == (4, pieces - 1):
+            take_gradients()
     for q in range(pieces):
         finish(flying[q])
         stores.append(

time: 41.1 us -> 42.3 us (1.029)
  Pallas kernels: 39.6 us -> 40.8 us
    pallas_call x1, Pallas kernels: 36.8 us -> 38 us  [body(): pl.pallas_call(functools.partial(kernel, nd, ns), out_shape=shapes[:2] +...]
where the time goes in v7:
time: 42.3 us; the launch traced here: 42.1 us
  Pallas kernels  40.8 us (96%)
  between operations  1.29 us (3%)
    pallas_call x1, Pallas kernels, body(): pl.pallas_call(functools.partial(kernel, nd, ns), out_shape=shapes[:2] +...  38 us
    pallas_call x1, Pallas kernels, body(): pl.pallas_call(writer, out_shape=shapes, in_specs=[hbm] * 3, out_specs=[h...  2.78 us

profile of v7, /device:TPU:0, one launch (start us, length us, event | category | flops | bytes accessed | tf_op | source)
XLA Modules:
  0.0 42.1 jit_solution(17938616760669766698)
XLA Ops:
  1.3 38.0 %shard_map.111 = (bf16[256,512]{1,0:T(8,128)(2,1)}, f32[256,512]{1,0:T(8,128)}, bf16[4,512,256]{2,1,0:T(8,128)(2,1)}) custom-call(bf16[256,512]{1,0:T(8,128)(2,1)} %features_hbm.1, bf16[512,512]{1,0:T(8,128)(2,1)} %w_self_hbm.1, bf16[512,512]{1,0:T(8,128)(2,1)} %w_neigh_hbm.1, bf16[256,512]{1,0:T(8,128)(2,1)} %cotangent_hbm.1, s32[32,256]{1,0:T(8,128)} %bitcast.2, ...), custom_call_target="tpu_custom_call" | custom-call | tf_op jit(solution)/shard_map/pallas_call | solution.py:473
  39.3 2.8 %shard_map.112 = (bf16[256,512]{1,0:T(8,128)(2,1)}, f32[256,512]{1,0:T(8,128)}, f32[512,512]{1,0:T(8,128)}, f32[512,512]{1,0:T(8,128)}) custom-call(bf16[256,512]{1,0:T(8,128)(2,1)} %get-tuple-element.7.hidden_in, f32[256,512]{1,0:T(8,128)} %get-tuple-element.8.grad_features_in, bf16[4,512,256]{2,1,0:T(8,128)(2,1)} %get-tuple-element.9.gathered_in), custom_call_target="tpu_custom_call" | custom-call | tf_op jit(solution)/shard_map/pallas_call | solution.py:530

commit v8 on v7

--- a/solution.py
+++ b/solution.py
@@ -385,11 +385,11 @@
         finish(flying[q])
         flying[q] = stage1(q)
     edge_gradients()
-    steps = [(8 * number + 5 * q, number, q) for number in range(2, 6) for q in range(pieces)]
+    steps = [(pieces * number + q, number, q) for number in range(2, 6) for q in range(pieces)]
     for _, number, q in sorted(steps):
         finish(flying[q])
         flying[q] = stages[number](q)
-        if (number, q) == (2, 1):
+        if (number, q) == (2, 0):
             send_gradients()
         if (number, q) == (2, pieces - 1):
             own_gradients()

time: 42.3 us -> 40.9 us (0.967)
  Pallas kernels: 40.8 us -> 39.4 us
    pallas_call x1, Pallas kernels: 38 us -> 36.6 us  [body(): pl.pallas_call(functools.partial(kernel, nd, ns), out_shape=shapes[:2] +...]
where the time goes in v8:
time: 40.9 us; the launch traced here: 40.7 us
  Pallas kernels  39.4 us (96%)
  between operations  1.29 us (3%)
    pallas_call x1, Pallas kernels, body(): pl.pallas_call(functools.partial(kernel, nd, ns), out_shape=shapes[:2] +...  36.6 us
    pallas_call x1, Pallas kernels, body(): pl.pallas_call(writer, out_shape=shapes, in_specs=[hbm] * 3, out_specs=[h...  2.78 us

profile of v8, /device:TPU:0, one launch (start us, length us, event | category | flops | bytes accessed | tf_op | source)
XLA Modules:
  0.0 40.7 jit_solution(2901803881852552018)
XLA Ops:
  1.3 36.6 %shard_map.111 = (bf16[256,512]{1,0:T(8,128)(2,1)}, f32[256,512]{1,0:T(8,128)}, bf16[4,512,256]{2,1,0:T(8,128)(2,1)}) custom-call(bf16[256,512]{1,0:T(8,128)(2,1)} %features_hbm.1, bf16[512,512]{1,0:T(8,128)(2,1)} %w_self_hbm.1, bf16[512,512]{1,0:T(8,128)(2,1)} %w_neigh_hbm.1, bf16[256,512]{1,0:T(8,128)(2,1)} %cotangent_hbm.1, s32[32,256]{1,0:T(8,128)} %bitcast.2, ...), custom_call_target="tpu_custom_call" | custom-call | tf_op jit(solution)/shard_map/pallas_call | solution.py:473
  37.9 2.8 %shard_map.112 = (bf16[256,512]{1,0:T(8,128)(2,1)}, f32[256,512]{1,0:T(8,128)}, f32[512,512]{1,0:T(8,128)}, f32[512,512]{1,0:T(8,128)}) custom-call(bf16[256,512]{1,0:T(8,128)(2,1)} %get-tuple-element.7.hidden_in, f32[256,512]{1,0:T(8,128)} %get-tuple-element.8.grad_features_in, bf16[4,512,256]{2,1,0:T(8,128)(2,1)} %get-tuple-element.9.gathered_in), custom_call_target="tpu_custom_call" | custom-call | tf_op jit(solution)/shard_map/pallas_call | solution.py:530
